TPU v7x, 128 devices: a whole 4x4x4 slice. The times are simulated.
128 devices in a mesh: loop: 16 (over y, z_lo, core), grp: 8 (over x, z_hi).
Axes of the slice: x: 4, y: 4, z: 4 (z_hi: 2, z_lo: 2; z = z_hi * 2 + z_lo), core: 2. Of those that a mesh axis runs over, the one named last changes fastest.
Arguments:
- patch_token_rows: bfloat16 [2048, 32, 1152], P(('loop', 'grp')), may hold values from -24 to 24
- probe_query_heads: float32 [1152], replicated, as said below
- key_value_matrix: bfloat16 [1152, 2304], replicated, may hold values from -0.1875 to 0.1875
- output_weight: bfloat16 [1152, 1152], replicated, may hold values from -0.1875 to 0.1875
- text_pooled_features: bfloat16 [2048, 1152], P(('loop', 'grp')), may hold values from -24 to 24
- text_head_weight: bfloat16 [1152, 1152], replicated, may hold values from -0.1875 to 0.1875
- log_logit_scale: float32 [1], replicated, may hold values from 4.2 to 4.8
- logit_bias_value: float32 [1], replicated, may hold values from -12 to -8
Outputs:
- grad_key_value: float32 [1152, 2304], P(('loop', 'grp'))
- grad_out: float32 [1152, 1152], P(('loop', 'grp'))
- grad_text: float32 [1152, 1152], P(('loop', 'grp'))
- grad_probe: float32 [1152], replicated
- text_feature_grad: bfloat16 [2048, 1152], P(('loop', 'grp'))
Inputs may be any that keep to these rules, and one draw needn't show every extreme that they name: `probe_query_heads`: entries are finite reals of either sign.
All inputs are finite; a program needn't handle non-finite values.
Results may differ from a plain program's by a relative error of at most 0.017.
The roundings to bfloat16 on the way count: a program that leaves them out, or rounds other values in their place, can miss the bound.
Values may be sent and summed in bfloat16 or wider, within the bound.
A program may use at most 128 MiB of HBM per device.

v0:
```python
import math

import jax
import jax.numpy as jnp
from jax import lax
from jax.sharding import PartitionSpec as P

HEADS = 16


def unit_rows(values):
    lengths = jnp.sqrt(jnp.sum(values * values, axis=1, keepdims=True) + 1e-06)
    return (values / lengths, lengths)


def unit_backward(gradient, unit, lengths):
    return (gradient - unit * jnp.sum(unit * gradient, axis=1, keepdims=True)) / lengths


def pair_weights_matrix(
    left_embedding, right_embedding, left_row_index, right_row_index, logit_scale, row_displacement
):
    similarity_scores = jnp.einsum(
        "id,jd->ij", left_embedding, right_embedding, preferred_element_type=jnp.float32
    )
    logit_matrix = logit_scale * similarity_scores + row_displacement
    pair_sign = jnp.where(left_row_index[:, None] == right_row_index[None, :], 1.0, -1.0).astype(
        jnp.float32
    )
    return (-pair_sign * jax.nn.sigmoid(-pair_sign * logit_matrix)).astype(jnp.bfloat16)


def shards(
    patch_token_rows,
    probe_query_heads,
    key_value_matrix,
    output_weight,
    text_pooled_features,
    text_head_weight,
    log_logit_scale,
    logit_bias_value,
):
    group_size = lax.axis_size("grp")
    loop_index = lax.axis_index("loop")
    own_index = loop_index * group_size + lax.axis_index("grp")
    local_images = text_pooled_features.shape[0]
    model_width = text_pooled_features.shape[1]
    patch_count = patch_token_rows.shape[1]
    head_width = model_width // HEADS
    score_root = math.sqrt(head_width)
    logit_scale = jnp.exp(log_logit_scale[0])
    row_displacement = logit_bias_value[0]
    text_out = jnp.dot(text_pooled_features, text_head_weight, preferred_element_type=jnp.float32)
    text_unit, text_lengths = unit_rows(text_out)
    text_local = text_unit.astype(jnp.bfloat16)
    text_block = lax.all_gather(text_local, "grp", axis=0, tiled=True)
    patch_rows = patch_token_rows.reshape(local_images * patch_count, model_width)
    key_values = jnp.dot(patch_rows, key_value_matrix, preferred_element_type=jnp.float32).astype(
        jnp.bfloat16
    )
    key_values = key_values.reshape(local_images, patch_count, 2, HEADS, head_width)
    key_part = key_values[:, :, 0]
    value_part = key_values[:, :, 1]
    query_half = probe_query_heads.astype(jnp.bfloat16).reshape(HEADS, head_width)
    scores = (
        jnp.einsum("nphe,he->nhp", key_part, query_half, preferred_element_type=jnp.float32)
        / score_root
    )
    weights = jax.nn.softmax(scores, axis=-1)
    weights_half = weights.astype(jnp.bfloat16)
    pooled = jnp.einsum(
        "nhp,nphe->nhe", weights_half, value_part, preferred_element_type=jnp.float32
    )
    pooled = pooled.astype(jnp.bfloat16).reshape(local_images, model_width)
    image_out = jnp.dot(pooled, output_weight, preferred_element_type=jnp.float32)
    image_unit, image_lengths = unit_rows(image_out)
    image_embedding = image_unit.astype(jnp.bfloat16)
    image_row_index = own_index * local_images + jnp.arange(local_images, dtype=jnp.int32)
    text_fragment = lax.all_gather(text_block, "loop", axis=0, tiled=True)
    text_row_index = jnp.arange(text_fragment.shape[0], dtype=jnp.int32)
    pair_factor = pair_weights_matrix(
        image_embedding,
        text_fragment,
        image_row_index,
        text_row_index,
        logit_scale,
        row_displacement,
    )
    image_portion = logit_scale * jnp.dot(
        pair_factor, text_fragment, preferred_element_type=jnp.float32
    )
    text_portion = logit_scale * jnp.einsum(
        "ij,id->jd", pair_factor, image_embedding, preferred_element_type=jnp.float32
    )
    image_portion, text_portion = (image_portion, text_portion)
    collected = text_portion
    image_handed_back, collected = (image_portion, collected)
    text_handed_back = lax.psum_scatter(collected, ("loop", "grp"), scatter_dimension=0, tiled=True)
    text_grad_out = unit_backward(text_handed_back, text_unit, text_lengths).astype(jnp.bfloat16)
    text_feature_grad = jnp.einsum(
        "ie,de->id", text_grad_out, text_head_weight, preferred_element_type=jnp.float32
    ).astype(jnp.bfloat16)
    text_term = jnp.einsum(
        "id,ie->de", text_pooled_features, text_grad_out, preferred_element_type=jnp.float32
    )
    image_grad_out = unit_backward(image_handed_back, image_unit, image_lengths).astype(
        jnp.bfloat16
    )
    out_term = jnp.einsum("id,ie->de", pooled, image_grad_out, preferred_element_type=jnp.float32)
    pooled_grad = jnp.einsum(
        "ie,de->id", image_grad_out, output_weight, preferred_element_type=jnp.float32
    ).astype(jnp.bfloat16)
    pooled_grad = pooled_grad.reshape(local_images, HEADS, head_width)
    weight_grad = jnp.einsum(
        "nhe,nphe->nhp", pooled_grad, value_part, preferred_element_type=jnp.float32
    )
    score_grad = (
        weights * (weight_grad - jnp.sum(weights * weight_grad, axis=-1, keepdims=True))
    ).astype(jnp.bfloat16)
    probe_term = (
        jnp.einsum("nhp,nphe->he", score_grad, key_part, preferred_element_type=jnp.float32)
        / score_root
    )
    key_grad = (
        jnp.swapaxes(score_grad, 1, 2).astype(jnp.float32)[..., None]
        * query_half.astype(jnp.float32)
        / score_root
    )
    value_grad = (
        jnp.swapaxes(weights_half, 1, 2).astype(jnp.float32)[..., None]
        * pooled_grad.astype(jnp.float32)[:, None]
    )
    kv_grad = jnp.stack([key_grad, value_grad], axis=2).astype(jnp.bfloat16)
    kv_grad = kv_grad.reshape(local_images * patch_count, 2 * model_width)
    grad_key_value = lax.psum_scatter(
        jnp.einsum("rd,re->de", patch_rows, kv_grad, preferred_element_type=jnp.float32),
        ("loop", "grp"),
        scatter_dimension=0,
        tiled=True,
    )
    grad_out, grad_text = (
        lax.psum_scatter(out_term, ("loop", "grp"), scatter_dimension=0, tiled=True),
        lax.psum_scatter(text_term, ("loop", "grp"), scatter_dimension=0, tiled=True),
    )
    grad_probe = lax.psum(probe_term.reshape(model_width), ("loop", "grp"))
    return (grad_key_value, grad_out, grad_text, grad_probe, text_feature_grad)


def solution(mesh):
    placed = (
        P(("loop", "grp"), None, None),
        P(),
        P(),
        P(),
        P(("loop", "grp"), None),
        P(),
        P(),
        P(),
    )
    return jax.shard_map(
        shards,
        mesh=mesh,
        in_specs=placed,
        out_specs=(
            P(("loop", "grp"), None),
            P(("loop", "grp"), None),
            P(("loop", "grp"), None),
            P(),
            P(("loop", "grp"), None),
        ),
        check_vma=False,
    )
```

profile of v0, /device:TPU:1, one launch (start us, length us, event | category | flops | bytes accessed | tf_op | source)
XLA Modules:
  0.0 999.4 jit_solution(5516795940712608894)
XLA Ops:
  7.2 2.5 multiply_reduce_fusion.2
  9.8 31.9 %all_gather.6 = bf16[128,1152]{1,0:T(8,128)(2,1)} all-gather(bf16[16,1152]{1,0:T(8,128)(2,1)S(1)} %fusion.32), channel_id=1, replica_groups=mesh['loop'=16,'grp'=8] {'grp'}, dimensions={0}, use_global_device_ids=true | all-gather | bytes 331776 | tf_op jit(solution)/shard_map/all_gather | solution.py:56
  41.8 7.5 convolution_convert_fusion
  49.3 11.3 %reshape.87 = bf16[16,32,2,16,72]{4,3,2,1,0:T(8,128)(2,1)} reshape(bf16[512,2304]{1,0:T(8,128)(2,1)} %convolution_convert_fusion) | data formatting | bytes 4718592 | tf_op jit(solution)/shard_map/reshape | solution.py:61
  60.7 3.1 slice_bitcast_fusion.1
  63.8 2.8 fusion.15
  67.1 0.7 fusion.11
  69.9 18.4 %all-gather.2.cloned.1.call-done = bf16[2048,1152]{1,0:T(8,128)(2,1)} async-done(((bf16[128,1152]{1,0:T(8,128)(2,1)}), bf16[2048,1152]{1,0:T(8,128)(2,1)}) %all-gather.2.cloned.1.call-update) | async-done | bytes 4718608 | tf_op jit(solution)/shard_map/all_gather | solution.py:79
  88.3 3.7 fusion.8
  92.0 5.1 convolution_multiply_fusion
  97.4 3.2 multiply_reduce_fusion.1
  100.6 0.8 convolution_convert_fusion.2
  101.8 2.8 fusion.9
  104.6 2.6 fusion.29
  107.5 1.4 multiply_convert_fusion.1
  108.9 1.3 multiply_convert_fusion
  110.2 2.9 pad_maximum_fusion
  113.1 7.0 convert_element_type.88
  120.1 3.2 fusion.33
  123.3 5.8 convolution_bitcast_fusion
  129.1 617.6 %reduce-scatter.4.cloned.1.call-done = f32[16,1152]{1,0:T(8,128)} async-done(((f32[2048,1152]{1,0:T(8,128)}), f32[16,1152]{1,0:T(8,128)}) %reduce-scatter.4.cloned.1.call-update) | async-done | bytes 73744 | tf_op jit(solution)/shard_map/reduce_scatter | solution.py:98
  746.7 1.1 multiply_reduce_fusion
  747.8 4.2 convolution_bitcast_fusion.1
  752.2 2.6 fusion.13
  754.9 72.7 %psum.7 = f32[1152]{0:T(1024)} all-reduce(f32[1152]{0:T(1024)S(1)} %reshape.91), channel_id=1, replica_groups=mesh['loop'=16,'grp'=8] {'loop','grp'}, use_global_device_ids=true, to_apply=%region_11.12 | all-reduce | flops 1152 | bytes 9216 | tf_op jit(solution)/shard_map/psum | solution.py:145
  827.6 1.5 convolution_convert_fusion.1
  829.0 154.4 %all-reduce.6.cloned.1.call-done = (f32[1152,2304]{0,1:T(8,128)}, f32[1152,1152]{1,0:T(8,128)}, f32[1152,1152]{0,1:T(8,128)}) async-done(((f32[1152,2304]{0,1:T(8,128)}, f32[1152,1152]{1,0:T(8,128)}, f32[1152,1152]{0,1:T(8,128)}), (f32[1152,2304]{0,1:T(8,128)}, f32[1152,1152]{1,0:T(8,128)}, f32[1152,1152]{0,1:T(8,128)})) %all-reduce.6.cloned.1.call-update) | async-done | bytes 21233680
  983.5 3.2 constant_dynamic-slice_fusion.2
  986.7 2.3 copy.23
  989.0 1.5 constant_dynamic-slice_fusion
  990.5 0.9 copy.24
  991.3 1.5 constant_dynamic-slice_fusion.1
  (46 shorter events, 2.8 us)
Async XLA Ops:
  7.2 62.1 %copy-start = (bf16[1152,1152]{1,0:T(8,128)(2,1)S(1)}, bf16[1152,1152]{1,0:T(8,128)(2,1)}, u32[]{:S(2)}) copy-start(bf16[1152,1152]{1,0:T(8,128)(2,1)} %param.11) | copy-start | bytes 7962628
  7.2 81.1 %all-gather.2.cloned.1.call-start = ((), (), s32[]{:S(2)}) async-start(), calls=%async_computation.1 | async-start | bytes 5013504 | tf_op jit(solution)/shard_map/all_gather | solution.py:79
  41.8 704.9 %reduce-scatter.4.cloned.1.call-start = ((), (), s32[]{:S(2)}) async-start(), calls=%async_computation.2 | async-start | bytes 9510912 | tf_op jit(solution)/shard_map/reduce_scatter | solution.py:98
  49.3 11.3 %copy-start.7 = (f32[1152]{0:T(1024)S(1)}, f32[1152]{0:T(1024)}, u32[]{:S(2)}) copy-start(f32[1152]{0:T(1024)} %param.9) | copy-start | bytes 13828
  63.8 4.0 copy-start.3
  63.8 4.0 copy-start.4
  97.1 886.4 %all-reduce.6.cloned.1.call-start = ((), (), s32[]{:S(2)}) async-start(), calls=%async_computation.3 | async-start | bytes 42467328
  120.1 3.2 copy-start.8
  123.3 624.5 %copy-start.6 = (bf16[16,1152]{1,0:T(8,128)(2,1)S(1)}, bf16[16,1152]{1,0:T(8,128)(2,1)}, u32[]{:S(2)}) copy-start(bf16[16,1152]{1,0:T(8,128)(2,1)} %param.12) | copy-start | bytes 110596
  752.0 75.6 %copy-start.2 = (bf16[1152,1152]{1,0:T(8,128)(2,1)S(1)}, bf16[1152,1152]{1,0:T(8,128)(2,1)}, u32[]{:S(2)}) copy-start(bf16[1152,1152]{1,0:T(8,128)(2,1)} %param.13) | copy-start | bytes 7962628
  752.0 75.6 %copy-start.5 = (f32[16,1152]{1,0:T(8,128)S(1)}, f32[16,1152]{1,0:T(8,128)}, u32[]{:S(2)}) copy-start(f32[16,1152]{1,0:T(8,128)} %reduce-scatter.4.cloned.1.call-done) | copy-start | bytes 221188
  983.5 9.4 copy-start.1
Sparse Core Ops, SparseCore 0:
  41.9 46.3 all-gather.1
  97.2 649.4 reduce-scatter.3
  752.9 230.5 all-reduce.5
where the time goes:
time: 1000 us; the launch traced here: 999 us
  waiting for transfers between devices  790 us (79%)
  blocking collectives  105 us (10%)
  matrix products  46.8 us (5%)
  local copies, waits for them, and re-layouts  31.9 us (3%)
  between operations  15.4 us (2%)
    reduce_scatter x1, waiting for transfers between devices, shards(): lax.psum_scatter(collected, ('loop', 'grp'), scatter_dimension=0, tiled=T...  618 us
    unnamed x4, waiting for transfers between devices  154 us
    psum x1, blocking collectives, shards(): grad_probe = lax.psum(probe_term.reshape(model_width), ('loop', 'grp'))  72.7 us
    all_gather x1, blocking collectives, shards(): text_block = lax.all_gather(text_local, 'grp', axis=0, tiled=True)  31.9 us
  transfers between devices with their start and end apart: 3, of which 3 were waited for; matrix products, arithmetic and copies ran while one was open for 6% of the time, Pallas kernels for 0%

commit v1 on v0

v1 whole, which is shorter than its diff:
```python
import functools
import math

import jax
import jax.numpy as jnp
from jax import lax
from jax.experimental import pallas as pl
from jax.experimental.pallas import tpu as pltpu
from jax.sharding import PartitionSpec as P

HEADS = 16
D = 1152
HEAD = D // HEADS
PATCH = 32
ROWS = 16
NL = 16
NG = 8
SLAB = D // NL
OWN = SLAB // NG
ROOT = math.sqrt(HEAD)
MESH = pl.DeviceIdType.MESH
F32 = jnp.float32
BF16 = jnp.bfloat16


def nn(a, b):
    return lax.dot_general(a, b, (((1,), (0,)), ((), ())), preferred_element_type=F32)


def nt(a, b):
    return lax.dot_general(a, b, (((1,), (1,)), ((), ())), preferred_element_type=F32)


def flip(a):
    return a.astype(F32).T.astype(BF16)


def iota(shape, dim):
    return lax.broadcasted_iota(jnp.int32, shape, dim)


def slab_of(values, place):
    block, shift = divmod(SLAB * place, 128)
    first = values[:, 128 * block : 128 * block + 128]
    if shift == 0:
        return first
    first = pltpu.roll(first, 128 - shift, 1)
    if shift + SLAB <= 128:
        return first
    second = pltpu.roll(values[:, 128 * block + 128 : 128 * block + 256], 128 - shift, 1)
    return jnp.where(iota(first.shape, 1) < 128 - shift, first, second)


def send_all(axis, count, me, source, target, send_sem, recv_sem):
    def one(step, carry):
        peer = lax.rem(me + step, count)
        pltpu.make_async_remote_copy(
            src_ref=source(peer),
            dst_ref=target.at[me],
            send_sem=send_sem,
            recv_sem=recv_sem,
            device_id={axis: peer},
            device_id_type=MESH,
        ).start()
        return carry

    lax.fori_loop(1, count, one, 0)


def all_but_one(axis, count, me, target, send_sem, recv_sem):
    part = target.at[pl.ds(0, count - 1)]
    return pltpu.make_async_remote_copy(
        src_ref=part,
        dst_ref=part,
        send_sem=send_sem,
        recv_sem=recv_sem,
        device_id={axis: lax.rem(me + 1, count)},
        device_id_type=MESH,
    )


def slot_sum(ref, count):
    total = ref[0].astype(F32)
    for slot in range(1, count):
        total = total + ref[slot].astype(F32)
    return total


def unit_backward(gradient, unit, length):
    return (gradient - unit * jnp.sum(unit * gradient, axis=1, keepdims=True)) / length


def kernel(
    scale_ref,
    bias_ref,
    probe_ref,
    text_ref,
    x_hbm,
    wkv_hbm,
    wout_hbm,
    wtext_hbm,
    gkv_ref,
    gout_ref,
    gtext_ref,
    gprobe_ref,
    gfeat_ref,
    x_ref,
    wkv_ref,
    wout_ref,
    wtext_ref,
    kv_ref,
    mask_ref,
    soft_ref,
    texts,
    images,
    slab_out,
    slab_in,
    iret_out,
    iret_in,
    tret_out,
    tret_in,
    tgo_all,
    igo_all,
    small_out,
    small_in,
    last_out,
    last_in,
    tiny_in,
    probe_rows,
    part_ref,
    last_f32,
    pgt_ref,
    gvt_ref,
    load_sem,
    send_sem,
    recv_sem,
):
    l = lax.axis_index("loop")
    k = lax.axis_index("grp")

    loads = [
        pltpu.make_async_copy(wtext_hbm, wtext_ref, load_sem.at[0]),
        pltpu.make_async_copy(x_hbm, x_ref, load_sem.at[1]),
        pltpu.make_async_copy(wkv_hbm, wkv_ref, load_sem.at[2]),
        pltpu.make_async_copy(wout_hbm, wout_ref, load_sem.at[3]),
    ]
    for load in loads:
        load.start()

    barrier = pltpu.get_barrier_semaphore()

    def greet(axis, count, me):
        def one(step, carry):
            pl.semaphore_signal(
                barrier, inc=1, device_id={axis: lax.rem(me + step, count)}, device_id_type=MESH
            )
            return carry

        lax.fori_loop(1, count, one, 0)

    greet("loop", NL, l)
    greet("grp", NG, k)

    def send_loop(phase, source, target):
        send_all("loop", NL, l, source, target, send_sem.at[phase], recv_sem.at[phase])

    def send_grp(phase, source, target):
        send_all("grp", NG, k, source, target, send_sem.at[phase], recv_sem.at[phase])

    def loop_copies(phase, target):
        return all_but_one("loop", NL, l, target, send_sem.at[phase], recv_sem.at[phase])

    def grp_copies(phase, target):
        return all_but_one("grp", NG, k, target, send_sem.at[phase], recv_sem.at[phase])

    head_of_row = iota((NL * ROWS, D), 0) >> 4
    column = iota((NL * ROWS, D), 1)
    in_head = (column >= head_of_row * HEAD) & (column < head_of_row * HEAD + HEAD)
    mask_ref[...] = jnp.where(in_head, 1.0, 0.0).astype(BF16)

    text_rows = text_ref[...].astype(F32)
    for place in range(NL):
        slab_out[place, (HEADS + 1) * ROWS :, :] = slab_of(text_rows, place).astype(BF16)

    loads[0].wait()
    text_out = nn(text_ref[...], wtext_ref[...])
    text_length = jnp.sqrt(jnp.sum(text_out * text_out, axis=1, keepdims=True) + 1e-06)
    text_unit = text_out / text_length
    texts[l] = text_unit.astype(BF16)
    pl.semaphore_wait(barrier, NL + NG - 2)
    send_loop(0, lambda p: texts.at[l], texts)

    loads[1].wait()
    loads[2].wait()

    def project(step, carry):
        columns = pl.ds(pl.multiple_of(step * 256, 256), 256)
        kv_ref[:, columns] = nn(x_ref[...], wkv_ref[:, columns]).astype(BF16)
        return carry

    lax.fori_loop(0, 2 * D // 256, project, 0)

    query = probe_ref[...].astype(BF16).astype(F32)
    query_heads = (mask_ref[...].astype(F32) * query).astype(BF16)
    same = (iota((ROWS * PATCH, HEADS * ROWS), 0) >> 5) == (
        iota((ROWS * PATCH, HEADS * ROWS), 1) & (ROWS - 1)
    )
    scores = nt(kv_ref[:, :D], query_heads) / ROOT
    highest = jnp.max(jnp.where(same, scores, -jnp.inf), axis=0, keepdims=True)
    powers = jnp.where(same, jnp.exp(scores - highest), 0.0)
    weights = powers / jnp.sum(powers, axis=0, keepdims=True)
    soft_ref[...] = weights
    weights_t = weights.T.astype(BF16)

    mixed = nn(weights_t, kv_ref[:, D:]) * mask_ref[...].astype(F32)
    pooled = jnp.sum(mixed.reshape(HEADS, ROWS, D), axis=0)
    pooled_half = pooled.astype(BF16)
    loads[3].wait()
    image_out = nn(pooled_half, wout_ref[...])
    image_length = jnp.sqrt(jnp.sum(image_out * image_out, axis=1, keepdims=True) + 1e-06)
    image_unit = image_out / image_length
    images[k] = image_unit.astype(BF16)
    send_grp(1, lambda p: images.at[k], images)

    part_ref[...] = nn(weights_t, x_ref[...])
    pooled_rows = pooled_half.astype(F32)
    for place in range(NL):
        slab_out[place, : HEADS * ROWS, :] = slab_of(part_ref[...], place).astype(BF16)
        slab_out[place, HEADS * ROWS : (HEADS + 1) * ROWS, :] = slab_of(pooled_rows, place).astype(
            BF16
        )
    slab_in[l] = slab_out[l]

    temperature = jnp.exp(scale_ref[...])
    loop_copies(0, texts).wait_recv()
    grp_copies(1, images).wait_recv()
    text_all = texts[...].reshape(NL * ROWS, D)
    image_all = images[...].reshape(NG * ROWS, D)
    logits = temperature * nt(image_all, text_all) + bias_ref[...]
    row = iota((NG * ROWS, NL * ROWS), 0)
    col = iota((NG * ROWS, NL * ROWS), 1)
    matched = ((row >> 4) == k) & ((col >> 4) == l) & ((row & 15) == (col & 15))
    sign = jnp.where(matched, 1.0, -1.0)
    coeff = -sign / (1.0 + jnp.exp(sign * logits))
    tret_out[...] = nn(flip(coeff), image_all).astype(BF16).reshape(NL, ROWS, D)
    tret_in[l] = tret_out[l]
    send_loop(2, lambda p: tret_out.at[p], tret_in)
    iret_out[...] = nn(coeff.astype(BF16), text_all).astype(BF16).reshape(NG, ROWS, D)
    iret_in[k] = iret_out[k]
    send_grp(3, lambda p: iret_out.at[p], iret_in)
    send_loop(4, lambda p: slab_out.at[p], slab_in)

    grp_copies(3, iret_in).wait_recv()
    image_returned = temperature * slot_sum(iret_in, NG)
    image_grad = unit_backward(image_returned, image_unit, image_length).astype(BF16)
    igo_all[l] = image_grad
    send_loop(5, lambda p: igo_all.at[l], igo_all)

    loop_copies(2, tret_in).wait_recv()
    text_returned = temperature * slot_sum(tret_in, NL)
    text_grad = unit_backward(text_returned, text_unit, text_length).astype(BF16)
    tgo_all[l] = text_grad
    send_loop(6, lambda p: tgo_all.at[l], tgo_all)

    pooled_grad = nt(image_grad, wout_ref[...]).astype(BF16).astype(F32)
    tiled = jnp.concatenate([pooled_grad] * HEADS, axis=0)
    grad_heads = (mask_ref[...].astype(F32) * tiled).astype(BF16)
    weight_grad = nt(kv_ref[:, D:], grad_heads)
    weights = soft_ref[...]
    inner = jnp.sum(weights * weight_grad, axis=0, keepdims=True)
    score_grad = (weights * (weight_grad - inner)).astype(BF16)
    fold = jnp.where((iota((HEADS * ROWS, 128), 0) >> 4) == iota((HEADS * ROWS, 128), 1), 1.0, 0.0)
    score_grad_t = nn(score_grad, fold.astype(BF16)).T[:HEADS].astype(BF16)
    key_sum = nn(score_grad_t, x_ref[...])
    head_row = iota((HEADS, D), 0)
    head_col = iota((HEADS, D), 1)
    own_head = (head_col >= head_row * HEAD) & (head_col < head_row * HEAD + HEAD)
    probe_sum = nn(score_grad_t, kv_ref[:, :D])
    probe_sum = jnp.sum(jnp.where(own_head, probe_sum, 0.0), axis=0, keepdims=True) / ROOT
    probe_rows[...] = jnp.zeros_like(probe_rows)
    for block in range(D // 128):
        probe_rows[block : block + 1, :] = probe_sum[:, 128 * block : 128 * block + 128]
    for place in range(NL):
        small_out[place, :HEADS, :] = slab_of(key_sum, place)
        small_out[place, HEADS:, :] = probe_rows[...]
    small_in[l] = small_out[l]
    send_loop(7, lambda p: small_out.at[p], small_in)

    gfeat_ref[...] = nt(text_grad, wtext_ref[...]).astype(BF16)

    last_f32[...] = jnp.zeros_like(last_f32)

    def place_rows(offset):
        for part in range(NG):
            last_f32[32 * part + offset : 32 * part + offset + OWN, :] = part_ref[
                OWN * part : OWN * part + OWN, :
            ]

    loop_copies(4, slab_in).wait_recv()
    loop_copies(5, igo_all).wait_recv()
    igo = igo_all[...].reshape(NL * ROWS, D)
    pgt_ref[...] = nt(wout_ref[...], igo).astype(BF16).astype(F32)
    for head in range(HEADS):
        left = pgt_ref[HEAD * head : HEAD * head + HEAD, :].astype(BF16)
        right = slab_in[:, ROWS * head : ROWS * head + ROWS, :].reshape(NL * ROWS, 128)
        gvt_ref[HEAD * head : HEAD * head + HEAD, :] = nn(left, right)
    part_ref[:128, :] = gvt_ref[...].T
    place_rows(2 * OWN)
    pooled_slab = slab_in[:, HEADS * ROWS : (HEADS + 1) * ROWS, :].reshape(NL * ROWS, 128)
    part_ref[:128, :] = nn(flip(pooled_slab), igo)
    place_rows(OWN)
    loop_copies(6, tgo_all).wait_recv()
    tgo = tgo_all[...].reshape(NL * ROWS, D)
    text_slab = slab_in[:, (HEADS + 1) * ROWS :, :].reshape(NL * ROWS, 128)
    part_ref[:128, :] = nn(flip(text_slab), tgo)
    place_rows(0)
    last_out[...] = last_f32[...].astype(BF16).reshape(NG, 32, D)
    last_in[k] = last_out[k]
    send_grp(8, lambda p: last_out.at[p], last_in)

    loop_copies(7, small_in).wait_recv()
    tiny_in[k] = slot_sum(small_in, NL)
    send_grp(9, lambda p: tiny_in.at[k], tiny_in)

    grp_copies(9, tiny_in).wait_recv()
    tiny = slot_sum(tiny_in, NG)
    for block in range(D // 128):
        gprobe_ref[:, 128 * block : 128 * block + 128] = tiny[HEADS + block : HEADS + block + 1, :]
    own_columns = pltpu.roll(tiny[:HEADS, :], lax.rem(128 - OWN * k, 128), 1)
    key_grad = lax.dot_general(
        own_columns.T,
        jnp.where(own_head, query, 0.0) / ROOT,
        (((1,), (0,)), ((), ())),
        preferred_element_type=F32,
        precision=lax.Precision.HIGHEST,
    )
    gkv_ref[:, :D] = key_grad[:OWN]

    grp_copies(8, last_in).wait_recv()
    last_f32[:32, :] = slot_sum(last_in, NG)
    gtext_ref[...] = last_f32[:OWN, :]
    gout_ref[...] = last_f32[OWN : 2 * OWN, :]
    gkv_ref[:, D:] = last_f32[2 * OWN : 3 * OWN, :]

    for phase, target in ((0, texts), (2, tret_in), (4, slab_in), (5, igo_all), (6, tgo_all), (7, small_in)):
        loop_copies(phase, target).wait_send()
    for phase, target in ((1, images), (3, iret_in), (8, last_in), (9, tiny_in)):
        grp_copies(phase, target).wait_send()


def shards(patches, probe, key_value_matrix, output_weight, text, text_weight, log_scale, bias):
    vmem = pl.BlockSpec(memory_space=pltpu.VMEM)
    anywhere = pl.BlockSpec(memory_space=pl.ANY)
    slab_rows = (HEADS + 2) * ROWS
    outs = pl.pallas_call(
        kernel,
        out_shape=(
            jax.ShapeDtypeStruct((OWN, 2 * D), F32),
            jax.ShapeDtypeStruct((OWN, D), F32),
            jax.ShapeDtypeStruct((OWN, D), F32),
            jax.ShapeDtypeStruct((1, D), F32),
            jax.ShapeDtypeStruct((ROWS, D), BF16),
        ),
        in_specs=[vmem] * 4 + [anywhere] * 4,
        out_specs=(vmem,) * 5,
        scratch_shapes=[
            pltpu.VMEM((ROWS * PATCH, D), BF16),
            pltpu.VMEM((D, 2 * D), BF16),
            pltpu.VMEM((D, D), BF16),
            pltpu.VMEM((D, D), BF16),
            pltpu.VMEM((ROWS * PATCH, 2 * D), BF16),
            pltpu.VMEM((HEADS * ROWS, D), BF16),
            pltpu.VMEM((ROWS * PATCH, HEADS * ROWS), F32),
            pltpu.VMEM((NL, ROWS, D), BF16),
            pltpu.VMEM((NG, ROWS, D), BF16),
            pltpu.VMEM((NL, slab_rows, 128), BF16),
            pltpu.VMEM((NL, slab_rows, 128), BF16),
            pltpu.VMEM((NG, ROWS, D), BF16),
            pltpu.VMEM((NG, ROWS, D), BF16),
            pltpu.VMEM((NL, ROWS, D), BF16),
            pltpu.VMEM((NL, ROWS, D), BF16),
            pltpu.VMEM((NL, ROWS, D), BF16),
            pltpu.VMEM((NL, ROWS, D), BF16),
            pltpu.VMEM((NL, 2 * HEADS, 128), F32),
            pltpu.VMEM((NL, 2 * HEADS, 128), F32),
            pltpu.VMEM((NG, 32, D), BF16),
            pltpu.VMEM((NG, 32, D), BF16),
            pltpu.VMEM((NG, 2 * HEADS, 128), F32),
            pltpu.VMEM((HEADS, 128), F32),
            pltpu.VMEM((HEADS * ROWS, D), F32),
            pltpu.VMEM((NG * 32, D), F32),
            pltpu.VMEM((D, NL * ROWS), F32),
            pltpu.VMEM((D, 128), F32),
            pltpu.SemaphoreType.DMA((4,)),
            pltpu.SemaphoreType.DMA((10,)),
            pltpu.SemaphoreType.DMA((10,)),
        ],
        compiler_params=pltpu.CompilerParams(
            collective_id=0, has_side_effects=True, vmem_limit_bytes=56 * 1024 * 1024
        ),
    )(
        log_scale.reshape(1, 1),
        bias.reshape(1, 1),
        probe.reshape(1, D),
        text,
        patches.reshape(ROWS * PATCH, D),
        key_value_matrix,
        output_weight,
        text_weight,
    )
    return outs[0], outs[1], outs[2], outs[3].reshape(D), outs[4]


def solution(mesh):
    rows = P(("loop", "grp"), None)
    return jax.shard_map(
        shards,
        mesh=mesh,
        in_specs=(P(("loop", "grp"), None, None), P(), P(), P(), rows, P(), P(), P()),
        out_specs=(rows, rows, rows, P(), rows),
        check_vma=False,
    )
```

time: 1000 us -> 86.1 us (0.09)
  waiting for transfers between devices: 790 us -> 0 us
  blocking collectives: 105 us -> 0 us
  Pallas kernels: 0 us -> 75.1 us
  matrix products: 46.8 us -> 0 us
  local copies, waits for them, and re-layouts: 31.9 us -> 7.3 us
  between operations: 15.4 us -> 1.93 us
    reduce_scatter x1 -> x0, waiting for transfers between devices: 618 us -> none  [shards(): lax.psum_scatter(collected, ('loop', 'grp'), scatter_dimension=0, tiled=T...]
    unnamed x4 -> x0, waiting for transfers between devices: 154 us -> none
    pallas_call x0 -> x1, Pallas kernels: none -> 75.1 us  [shards(): pl.pallas_call(kernel, out_shape=(jax.ShapeDtypeStruct((OWN, 2 * D), F32)...]
    psum x1 -> x0, blocking collectives: 72.7 us -> none  [shards(): grad_probe = lax.psum(probe_term.reshape(model_width), ('loop', 'grp'))]
    dot_general x15 -> x0, matrix products: 46.8 us -> none  [the longest x1 7.52 us: shards(): jnp.dot(patch_rows, key_value_matrix, preferred_element_type=jnp.float32)]
    all_gather x1 -> x0, blocking collectives: 31.9 us -> none  [shards(): text_block = lax.all_gather(text_local, 'grp', axis=0, tiled=True)]
    all_gather x1 -> x0, waiting for transfers between devices: 18.4 us -> none  [shards(): text_fragment = lax.all_gather(text_block, 'loop', axis=0, tiled=True)]
    reshape x7 -> x1, local copies, waits for them, and re-layouts: 12.1 us -> 1.29 us  [shards(): probe.reshape(1, D)]
  transfers between devices with their start and end apart: 3 -> 0, of which waited for: 3 -> 0; matrix products, arithmetic and copies ran while one was open for 6% -> 0% of each run, Pallas kernels for 0% -> 0%
where the time goes in v1:
time: 86.1 us; the launch traced here: 85.7 us
  Pallas kernels  75.1 us (87%)
  local copies, waits for them, and re-layouts  7.3 us (8%)
  between operations  1.93 us (2%)
  other arithmetic  1.31 us (2%)
    pallas_call x1, Pallas kernels, shards(): pl.pallas_call(kernel, out_shape=(jax.ShapeDtypeStruct((OWN, 2 * D), F32)...  75.1 us
    unnamed x4, local copies, waits for them, and re-layouts  6.01 us

profile of v1, /device:TPU:1, one launch (start us, length us, event | category | flops | bytes accessed | tf_op | source)
XLA Modules:
  0.0 85.7 jit_solution(17422068303911764240)
XLA Ops:
  1.9 1.3 %reshape.27.probe_ref = f32[1,1152]{1,0:T(1,128)} reshape(f32[1152]{0:T(1024)} %param.9) | data formatting | bytes 9216 | tf_op jit(solution)/shard_map/reshape | solution.py:404
  3.2 75.1 %shard_map.119 = (f32[9,2304]{1,0:T(8,128)}, f32[9,1152]{1,0:T(8,128)}, f32[9,1152]{1,0:T(8,128)}, f32[1,1152]{1,0:T(1,128)}, bf16[16,1152]{1,0:T(8,128)(2,1)}) custom-call(f32[1,1]{1,0:T(1,128)} %bitcast.3.scale_ref, f32[1,1]{1,0:T(1,128)} %bitcast.4.bias_ref, f32[1,1152]{1,0:T(1,128)} %reshape.27.probe_ref, bf16[16,1152]{1,0:T(8,128)(2,1)} %text_ref.1, ...), custom_call_target="tpu_custom_call" | custom-call | tf_op jit(solution)/shard_map/pallas_call | solution.py:355
  78.3 1.3 %reduce = f32[1152]{0:T(1024)} reduce(f32[1,1152]{1,0:T(1,128)} %get-tuple-element.13, f32[]{:T(128)} %constant.2), dimensions={0}, to_apply=%get-tuple-element.13.reduce_sub_computation | reduce | bytes 9220 | tf_op jit(solution)/shard_map/pallas_call | solution.py:355
  79.6 1.6 %copy.19 = f32[9,2304]{1,0:T(8,128)} copy(f32[9,2304]{1,0:T(8,128)} %get-tuple-element.20) | data formatting | bytes 165888
  81.2 1.5 %copy.20 = f32[9,1152]{1,0:T(8,128)} copy(f32[9,1152]{1,0:T(8,128)} %get-tuple-element.21) | data formatting | bytes 82944
  82.7 1.5 %copy.21 = f32[9,1152]{1,0:T(8,128)} copy(f32[9,1152]{1,0:T(8,128)} %get-tuple-element.22) | data formatting | bytes 82944
  84.3 1.4 %copy.22 = bf16[16,1152]{1,0:T(8,128)(2,1)} copy(bf16[16,1152]{1,0:T(8,128)(2,1)} %get-tuple-element.24) | data formatting | bytes 73728

commit v2 on v1

v2 whole, which is shorter than its diff:
```python
import functools
import math

import jax
import jax.numpy as jnp
import ml_dtypes
import numpy as np
from jax import lax
from jax.experimental import pallas as pl
from jax.experimental.pallas import tpu as pltpu
from jax.sharding import PartitionSpec as P

HEADS = 16
D = 1152
HEAD = D // HEADS
PATCH = 32
ROWS = 16
NC = 8
NP = 16
SLAB = D // NC
OWN = SLAB // NP
SPARE = SLAB - 128
ROOT = math.sqrt(HEAD)
MESH = pl.DeviceIdType.MESH
F32 = jnp.float32
BF16 = jnp.bfloat16


def nn(a, b):
    return lax.dot_general(a, b, (((1,), (0,)), ((), ())), preferred_element_type=F32)


def nt(a, b):
    return lax.dot_general(a, b, (((1,), (1,)), ((), ())), preferred_element_type=F32)


def flip(a):
    return a.astype(F32).T.astype(BF16)


def iota(shape, dim):
    return lax.broadcasted_iota(jnp.int32, shape, dim)


def slab_of(values, start):
    block, shift = divmod(start, 128)
    first = values[:, 128 * block : 128 * block + 128]
    if shift == 0:
        return first
    first = pltpu.roll(first, 128 - shift, 1)
    if 128 * block + 128 >= values.shape[1]:
        return first
    second = pltpu.roll(values[:, 128 * block + 128 : 128 * block + 256], 128 - shift, 1)
    return jnp.where(iota(first.shape, 1) < 128 - shift, first, second)


def send_all(peer_of, count, me, source, target, send_sem, recv_sem):
    def one(step, carry):
        peer = lax.rem(me + step, count)
        pltpu.make_async_remote_copy(
            src_ref=source(peer),
            dst_ref=target(me),
            send_sem=send_sem,
            recv_sem=recv_sem,
            device_id=peer_of(peer),
            device_id_type=MESH,
        ).start()
        return carry

    lax.fori_loop(1, count, one, 0)


def all_but_one(peer_of, count, me, target, send_sem, recv_sem):
    part = target(pl.ds(0, count - 1))
    return pltpu.make_async_remote_copy(
        src_ref=part,
        dst_ref=part,
        send_sem=send_sem,
        recv_sem=recv_sem,
        device_id=peer_of(lax.rem(me + 1, count)),
        device_id_type=MESH,
    )


def slot_sum(ref, count):
    total = ref[0].astype(F32)
    for slot in range(1, count):
        total = total + ref[slot].astype(F32)
    return total


def unit_backward(gradient, unit, length):
    return (gradient - unit * jnp.sum(unit * gradient, axis=1, keepdims=True)) / length


def kernel(
    scale_ref,
    bias_ref,
    probe_ref,
    text_ref,
    x_hbm,
    wkv_hbm,
    wout_hbm,
    wtext_hbm,
    order_hbm,
    gkv_ref,
    gout_ref,
    gtext_ref,
    gprobe_ref,
    gfeat_ref,
    x_ref,
    wkv_ref,
    wout_ref,
    wtext_ref,
    order_ref,
    kv_ref,
    mask_ref,
    soft_ref,
    texts,
    images,
    slab_out,
    slab_in,
    iret_out,
    iret_in,
    tret_out,
    tret_in,
    tgo_all,
    igo_all,
    small_out,
    small_in,
    last_out,
    last_in,
    tiny_out,
    tiny_in,
    part_ref,
    last_f32,
    heads_ref,
    load_sem,
    send_sem,
    recv_sem,
):
    l = lax.axis_index("loop")
    k = lax.axis_index("grp")
    c = (k % 2) * 4 + l % 4
    s = (l // 4) * 4 + k // 2

    def in_column(peer):
        return {"loop": (l // 4) * 4 + peer % 4, "grp": (k // 2) * 2 + peer // 4}

    def in_plane(peer):
        return {"loop": (peer // 4) * 4 + l % 4, "grp": (peer % 4) * 2 + k % 2}

    loads = [
        pltpu.make_async_copy(wtext_hbm, wtext_ref, load_sem.at[0]),
        pltpu.make_async_copy(x_hbm, x_ref, load_sem.at[1]),
        pltpu.make_async_copy(wkv_hbm, wkv_ref, load_sem.at[2]),
        pltpu.make_async_copy(wout_hbm, wout_ref, load_sem.at[3]),
        pltpu.make_async_copy(order_hbm, order_ref, load_sem.at[4]),
    ]
    for load in loads:
        load.start()

    barrier = pltpu.get_barrier_semaphore()

    def greet(peer_of, count, me):
        def one(step, carry):
            peer = peer_of(lax.rem(me + step, count))
            pl.semaphore_signal(barrier, inc=1, device_id=peer, device_id_type=MESH)
            return carry

        lax.fori_loop(1, count, one, 0)

    greet(in_plane, NP, s)
    greet(in_column, NC, c)

    column = (in_column, NC, c)
    plane = (in_plane, NP, s)
    phases = {
        0: (plane, lambda i: texts.at[i]),
        1: (column, lambda i: images.at[i]),
        2: (plane, lambda i: tret_in.at[i]),
        3: (column, lambda i: iret_in.at[i]),
        4: (column, lambda i: slab_in.at[i]),
        5: (column, lambda i: igo_all.at[i]),
        6: (column, lambda i: tgo_all.at[i]),
        7: (column, lambda i: small_in.at[i]),
        8: (plane, lambda i: last_in.at[0, i]),
        9: (plane, lambda i: last_in.at[1, i]),
        10: (plane, lambda i: tiny_in.at[i]),
    }
    started = []

    def copies(phase):
        (peer_of, count, me), target = phases[phase]
        return all_but_one(peer_of, count, me, target, send_sem.at[phase], recv_sem.at[phase])

    def send(phase, source):
        (peer_of, count, me), target = phases[phase]
        send_all(peer_of, count, me, source, target, send_sem.at[phase], recv_sem.at[phase])
        started.append(phase)

    def arrive(phase):
        copies(phase).wait_recv()

    head_of_row = iota((HEADS * ROWS, D), 0) >> 4
    lane = iota((HEADS * ROWS, D), 1)
    in_head = (lane >= head_of_row * HEAD) & (lane < head_of_row * HEAD + HEAD)
    mask_ref[...] = jnp.where(in_head, 1.0, 0.0).astype(BF16)

    loads[0].wait()
    text_out = nn(text_ref[...], wtext_ref[...])
    text_length = jnp.sqrt(jnp.sum(text_out * text_out, axis=1, keepdims=True) + 1e-06)
    text_unit = text_out / text_length
    texts[s] = text_unit.astype(BF16)
    pl.semaphore_wait(barrier, NP + NC - 2)
    send(0, lambda p: texts.at[s])

    loads[1].wait()
    loads[2].wait()

    def project(step, carry):
        columns = pl.ds(pl.multiple_of(step * 256, 256), 256)
        kv_ref[:, columns] = nn(x_ref[...], wkv_ref[:, columns]).astype(BF16)
        return carry

    lax.fori_loop(0, 2 * D // 256, project, 0)

    query = probe_ref[...].astype(BF16).astype(F32)
    query_heads = (mask_ref[...].astype(F32) * query).astype(BF16)
    same = (iota((ROWS * PATCH, HEADS * ROWS), 0) >> 5) == (
        iota((ROWS * PATCH, HEADS * ROWS), 1) & (ROWS - 1)
    )
    scores = nt(kv_ref[:, :D], query_heads) / ROOT
    highest = jnp.max(jnp.where(same, scores, -jnp.inf), axis=0, keepdims=True)
    powers = jnp.where(same, jnp.exp(scores - highest), 0.0)
    weights = powers / jnp.sum(powers, axis=0, keepdims=True)
    soft_ref[...] = weights
    weights_t = weights.T.astype(BF16)

    mixed = nn(weights_t, kv_ref[:, D:]) * mask_ref[...].astype(F32)
    pooled = jnp.sum(mixed.reshape(HEADS, ROWS, D), axis=0)
    pooled_half = pooled.astype(BF16)
    loads[3].wait()
    image_out = nn(pooled_half, wout_ref[...])
    image_length = jnp.sqrt(jnp.sum(image_out * image_out, axis=1, keepdims=True) + 1e-06)
    image_unit = image_out / image_length
    images[c] = image_unit.astype(BF16)
    send(1, lambda p: images.at[c])

    patch_sums = nn(weights_t, x_ref[...]).astype(BF16)
    features = jnp.concatenate([pooled_half, text_ref[...]], axis=0)
    loads[4].wait()

    for place in range(NC):
        rows = order_ref[SLAB * place : SLAB * place + SLAB, :]
        slab_out[place, :SLAB, :] = nt(rows, patch_sums).astype(BF16)
        slab_out[place, SLAB:, :SLAB] = nt(features, rows).astype(BF16)
    slab_in[c] = slab_out[c]

    temperature = jnp.exp(scale_ref[...])
    arrive(0)
    arrive(1)
    text_all = texts[...].reshape(NP * ROWS, D)
    image_all = images[...].reshape(NC * ROWS, D)
    logits = temperature * nt(image_all, text_all) + bias_ref[...]
    row = iota((NC * ROWS, NP * ROWS), 0)
    col = iota((NC * ROWS, NP * ROWS), 1)
    matched = ((row >> 4) == c) & ((col >> 4) == s) & ((row & 15) == (col & 15))
    sign = jnp.where(matched, 1.0, -1.0)
    coeff = -sign / (1.0 + jnp.exp(sign * logits))
    tret_out[...] = nn(flip(coeff), image_all).astype(BF16).reshape(NP, ROWS, D)
    tret_in[s] = tret_out[s]
    send(2, lambda p: tret_out.at[p])
    iret_out[...] = nn(coeff.astype(BF16), text_all).astype(BF16).reshape(NC, ROWS, D)
    iret_in[c] = iret_out[c]
    send(3, lambda p: iret_out.at[p])
    send(4, lambda p: slab_out.at[p])

    arrive(3)
    image_returned = temperature * slot_sum(iret_in, NC)
    image_grad = unit_backward(image_returned, image_unit, image_length).astype(BF16)
    igo_all[c] = image_grad
    send(5, lambda p: igo_all.at[c])

    pooled_grad = nt(image_grad, wout_ref[...]).astype(BF16).astype(F32)
    tiled = jnp.concatenate([pooled_grad] * HEADS, axis=0)
    grad_heads = (mask_ref[...].astype(F32) * tiled).astype(BF16)
    weight_grad = nt(kv_ref[:, D:], grad_heads)
    weights = soft_ref[...]
    inner = jnp.sum(weights * weight_grad, axis=0, keepdims=True)
    score_grad = (weights * (weight_grad - inner)).astype(BF16)
    fold = jnp.where((iota((HEADS * ROWS, 128), 0) >> 4) == iota((HEADS * ROWS, 128), 1), 1.0, 0.0)
    score_grad_t = nn(score_grad, fold.astype(BF16)).T[:HEADS].astype(BF16)

    key_sum = nn(score_grad_t, x_ref[...])
    high = key_sum.astype(BF16)
    low = (key_sum - high.astype(F32)).astype(BF16)
    key_sum = jnp.concatenate([high, low], axis=0)
    head_row = iota((HEADS, D), 0)
    head_col = iota((HEADS, D), 1)
    own_head = (head_col >= head_row * HEAD) & (head_col < head_row * HEAD + HEAD)
    probe_sum = jnp.where(own_head, nn(score_grad_t, kv_ref[:, :D]), 0.0) / ROOT
    tile_row = iota((HEADS, 128), 0)
    tile_lane = iota((HEADS, 128), 1)
    probe_tile = jnp.zeros((HEADS, 128), F32)
    for head in range(HEADS):
        probe_tile = jnp.where(tile_row == head, slab_of(probe_sum, HEAD * head), probe_tile)
    probe_tile = pltpu.roll(probe_tile, SPARE, 1)
    for place in range(NC):
        rows = order_ref[SLAB * place : SLAB * place + SLAB, :]
        split = nt(key_sum, rows)
        small_out[place, :, :SLAB] = split[:HEADS] + split[HEADS:]
        small_out[place, :, 128:] = jnp.where(
            tile_lane < SPARE, small_out[place, :, 128:], probe_tile
        )
    small_in[c] = small_out[c]
    send(7, lambda p: small_out.at[p])

    arrive(2)
    text_returned = temperature * slot_sum(tret_in, NP)
    text_grad = unit_backward(text_returned, text_unit, text_length).astype(BF16)
    tgo_all[c] = text_grad
    send(6, lambda p: tgo_all.at[c])

    last_f32[...] = jnp.zeros_like(last_f32)

    def place_rows(offset):
        for part in range(NP):
            last_f32[32 * part + offset : 32 * part + offset + OWN, :] = part_ref[
                OWN * part : OWN * part + OWN, :
            ]

    arrive(4)
    arrive(5)
    igo = igo_all[...].reshape(NC * ROWS, D)
    part_ref[...] = nn(flip(slab_in[:, SLAB : SLAB + ROWS, :].reshape(NC * ROWS, 256))[:SLAB], igo)
    place_rows(0)
    pooled_grads = nt(igo, wout_ref[...]).astype(BF16)
    for place in range(NC):
        tiled = jnp.concatenate([pooled_grads[ROWS * place : ROWS * place + ROWS]] * HEADS, axis=0)
        heads_ref[256 * place : 256 * place + 256, :] = mask_ref[...] * tiled
    left = jnp.concatenate([slab_in[place, :SLAB, :] for place in range(NC)], axis=1)
    part_ref[...] = nn(left, heads_ref[...])
    place_rows(OWN)

    def pack(half):
        rows = last_f32[...].reshape(NP, 32, D)[:, 16 * half : 16 * half + 16]
        last_out[half] = rows.astype(BF16)
        last_in[half, s] = last_out[half, s]

    pack(0)
    send(8, lambda p: last_out.at[0, p])

    arrive(7)
    tiny = slot_sum(small_in, NC)
    for place in range(NP):
        tiny_out[place] = jnp.where(
            tile_lane < SPARE, slab_of(tiny, OWN * place), tiny[:, 128:]
        )
    tiny_in[s] = tiny_out[s]
    send(10, lambda p: tiny_out.at[p])

    arrive(6)
    tgo = tgo_all[...].reshape(NC * ROWS, D)
    part_ref[...] = nn(flip(slab_in[:, SLAB + ROWS :, :].reshape(NC * ROWS, 256))[:SLAB], tgo)
    place_rows(2 * OWN)
    pack(1)
    send(9, lambda p: last_out.at[1, p])

    gfeat_ref[...] = nt(text_grad, wtext_ref[...]).astype(BF16)

    arrive(10)
    tiny = slot_sum(tiny_in, NP)
    gprobe_ref[...] = pltpu.roll(tiny, 128 - SPARE, 1)[:, :HEAD]
    key_grad = lax.dot_general(
        tiny.T[:16, :],
        jnp.where(own_head, query, 0.0) / ROOT,
        (((1,), (0,)), ((), ())),
        preferred_element_type=F32,
        precision=lax.Precision.HIGHEST,
    )
    gkv_ref[:, :D] = key_grad[:OWN]

    arrive(8)
    last_f32[:16, :] = slot_sum(last_in.at[0], NP)
    arrive(9)
    last_f32[16:32, :] = slot_sum(last_in.at[1], NP)
    gout_ref[...] = last_f32[:OWN, :]
    gkv_ref[:, D:] = last_f32[OWN : 2 * OWN, :]
    gtext_ref[...] = last_f32[2 * OWN : 3 * OWN, :]

    for phase in started:
        copies(phase).wait_send()


def column_order():
    c, s, r = np.meshgrid(np.arange(NC), np.arange(NP), np.arange(OWN), indexing="ij")
    loop = (s // 4) * 4 + c % 4
    grp = (s % 4) * 2 + c // 4
    kept = ((loop * 8 + grp) * OWN + r).reshape(D)
    return (kept[:, None] == np.arange(D)[None, :]).astype(ml_dtypes.bfloat16)


def shards(patches, probe, key_value_matrix, output_weight, text, text_weight, log_scale, bias):
    vmem = pl.BlockSpec(memory_space=pltpu.VMEM)
    anywhere = pl.BlockSpec(memory_space=pl.ANY)
    outs = pl.pallas_call(
        kernel,
        out_shape=(
            jax.ShapeDtypeStruct((OWN, 2 * D), F32),
            jax.ShapeDtypeStruct((OWN, D), F32),
            jax.ShapeDtypeStruct((OWN, D), F32),
            jax.ShapeDtypeStruct((HEADS, HEAD), F32),
            jax.ShapeDtypeStruct((ROWS, D), BF16),
        ),
        in_specs=[vmem] * 4 + [anywhere] * 5,
        out_specs=(vmem,) * 5,
        scratch_shapes=[
            pltpu.VMEM((ROWS * PATCH, D), BF16),
            pltpu.VMEM((D, 2 * D), BF16),
            pltpu.VMEM((D, D), BF16),
            pltpu.VMEM((D, D), BF16),
            pltpu.VMEM((D, D), BF16),
            pltpu.VMEM((ROWS * PATCH, 2 * D), BF16),
            pltpu.VMEM((HEADS * ROWS, D), BF16),
            pltpu.VMEM((ROWS * PATCH, HEADS * ROWS), F32),
            pltpu.VMEM((NP, ROWS, D), BF16),
            pltpu.VMEM((NC, ROWS, D), BF16),
            pltpu.VMEM((NC, SLAB + 2 * ROWS, HEADS * ROWS), BF16),
            pltpu.VMEM((NC, SLAB + 2 * ROWS, HEADS * ROWS), BF16),
            pltpu.VMEM((NC, ROWS, D), BF16),
            pltpu.VMEM((NC, ROWS, D), BF16),
            pltpu.VMEM((NP, ROWS, D), BF16),
            pltpu.VMEM((NP, ROWS, D), BF16),
            pltpu.VMEM((NC, ROWS, D), BF16),
            pltpu.VMEM((NC, ROWS, D), BF16),
            pltpu.VMEM((NC, HEADS, 256), F32),
            pltpu.VMEM((NC, HEADS, 256), F32),
            pltpu.VMEM((2, NP, 16, D), BF16),
            pltpu.VMEM((2, NP, 16, D), BF16),
            pltpu.VMEM((NP, HEADS, 128), F32),
            pltpu.VMEM((NP, HEADS, 128), F32),
            pltpu.VMEM((SLAB, D), F32),
            pltpu.VMEM((NP * 32, D), F32),
            pltpu.VMEM((NC * HEADS * ROWS, D), BF16),
            pltpu.SemaphoreType.DMA((5,)),
            pltpu.SemaphoreType.DMA((11,)),
            pltpu.SemaphoreType.DMA((11,)),
        ],
        compiler_params=pltpu.CompilerParams(
            collective_id=0, has_side_effects=True, vmem_limit_bytes=56 * 1024 * 1024
        ),
    )(
        log_scale.reshape(1, 1),
        bias.reshape(1, 1),
        probe.reshape(1, D),
        text,
        patches.reshape(ROWS * PATCH, D),
        key_value_matrix,
        output_weight,
        text_weight,
        jnp.asarray(column_order()),
    )
    return outs[0], outs[1], outs[2], outs[3].reshape(D), outs[4]


def solution(mesh):
    rows = P(("loop", "grp"), None)
    return jax.shard_map(
        shards,
        mesh=mesh,
        in_specs=(P(("loop", "grp"), None, None), P(), P(), P(), rows, P(), P(), P()),
        out_specs=(rows, rows, rows, P(), rows),
        check_vma=False,
    )
```

time: 86.1 us -> 71.4 us (0.83)
  Pallas kernels: 75.1 us -> 60.3 us
  local copies, waits for them, and re-layouts: 7.3 us -> 8.68 us
  other arithmetic: 1.31 us -> 0 us
    pallas_call x1, Pallas kernels: 75.1 us -> 60.3 us  [shards(): pl.pallas_call(kernel, out_shape=(jax.ShapeDtypeStruct((OWN, 2 * D), F32)...]
    reshape x0 -> x1, local copies, waits for them, and re-layouts: none -> 1.38 us  [shards(): return (outs[0], outs[1], outs[2], outs[3].reshape(D), outs[4])]
    pallas_call x1 -> x0, other arithmetic: 1.31 us -> none  [shards(): pl.pallas_call(kernel, out_shape=(jax.ShapeDtypeStruct((OWN, 2 * D), F32)...]
where the time goes in v2:
time: 71.4 us; the launch traced here: 71 us
  Pallas kernels  60.3 us (84%)
  local copies, waits for them, and re-layouts  8.68 us (12%)
  between operations  1.93 us (3%)
    pallas_call x1, Pallas kernels, shards(): pl.pallas_call(kernel, out_shape=(jax.ShapeDtypeStruct((OWN, 2 * D), F32)...  60.3 us
    unnamed x4, local copies, waits for them, and re-layouts  6.01 us

profile of v2, /device:TPU:1, one launch (start us, length us, event | category | flops | bytes accessed | tf_op | source)
XLA Modules:
  0.0 71.0 jit_solution(12284584038969644275)
XLA Ops:
  1.9 1.3 %reshape.27.probe_ref = f32[1,1152]{1,0:T(1,128)} reshape(f32[1152]{0:T(1024)} %param.10) | data formatting | bytes 9216 | tf_op jit(solution)/shard_map/reshape | solution.py:456
  3.2 60.3 %shard_map.128 = (f32[9,2304]{1,0:T(8,128)}, f32[9,1152]{1,0:T(8,128)}, f32[9,1152]{1,0:T(8,128)}, f32[16,72]{1,0:T(8,128)}, bf16[16,1152]{1,0:T(8,128)(2,1)}) custom-call(f32[1,1]{1,0:T(1,128)} %bitcast.3.scale_ref, f32[1,1]{1,0:T(1,128)} %bitcast.4.bias_ref, f32[1,1152]{1,0:T(1,128)} %reshape.27.probe_ref, bf16[16,1152]{1,0:T(8,128)(2,1)} %text_ref.1, ...), custom_call_target="tpu_custom_call" | custom-call | tf_op jit(solution)/shard_map/pallas_call | solution.py:407
  63.6 1.4 %reshape.29 = f32[1152]{0:T(1024)} reshape(f32[16,72]{1,0:T(8,128)} %get-tuple-element.13) | data formatting | bytes 9216 | tf_op jit(solution)/shard_map/reshape | solution.py:464
  64.9 1.6 %copy.20 = f32[9,2304]{1,0:T(8,128)} copy(f32[9,2304]{1,0:T(8,128)} %get-tuple-element.20) | data formatting | bytes 165888
  66.5 1.5 %copy.21 = f32[9,1152]{1,0:T(8,128)} copy(f32[9,1152]{1,0:T(8,128)} %get-tuple-element.21) | data formatting | bytes 82944
  68.0 1.5 %copy.22 = f32[9,1152]{1,0:T(8,128)} copy(f32[9,1152]{1,0:T(8,128)} %get-tuple-element.22) | data formatting | bytes 82944
  69.6 1.4 %copy.23 = bf16[16,1152]{1,0:T(8,128)(2,1)} copy(bf16[16,1152]{1,0:T(8,128)(2,1)} %get-tuple-element.24) | data formatting | bytes 73728

commit v3 on v2

--- a/solution.py
+++ b/solution.py
@@ -38,6 +38,16 @@
     return a.astype(F32).T.astype(BF16)
 
 
+def exact(a, b):
+    return lax.dot_general(
+        a,
+        b,
+        (((1,), (0,)), ((), ())),
+        preferred_element_type=F32,
+        precision=lax.Precision.HIGHEST,
+    )
+
+
 def iota(shape, dim):
     return lax.broadcasted_iota(jnp.int32, shape, dim)
 
@@ -103,17 +113,15 @@
     wout_hbm,
     wtext_hbm,
     order_hbm,
-    gkv_ref,
-    gout_ref,
-    gtext_ref,
-    gprobe_ref,
+    sums_ref,
     gfeat_ref,
     x_ref,
-    wkv_ref,
+    wk_ref,
+    keys_ref,
+    wv_ref,
     wout_ref,
     wtext_ref,
     order_ref,
-    kv_ref,
     mask_ref,
     soft_ref,
     texts,
@@ -150,15 +158,19 @@
     def in_plane(peer):
         return {"loop": (peer // 4) * 4 + l % 4, "grp": (peer % 4) * 2 + k % 2}
 
+    def load(source, target, number):
+        return pltpu.make_async_copy(source, target, load_sem.at[number])
+
     loads = [
-        pltpu.make_async_copy(wtext_hbm, wtext_ref, load_sem.at[0]),
-        pltpu.make_async_copy(x_hbm, x_ref, load_sem.at[1]),
-        pltpu.make_async_copy(wkv_hbm, wkv_ref, load_sem.at[2]),
-        pltpu.make_async_copy(wout_hbm, wout_ref, load_sem.at[3]),
-        pltpu.make_async_copy(order_hbm, order_ref, load_sem.at[4]),
+        load(wtext_hbm, wtext_ref, 0),
+        load(wkv_hbm.at[:, :D], wk_ref, 1),
+        load(x_hbm, x_ref, 2),
+        load(wkv_hbm.at[:, D:], wv_ref, 3),
+        load(wout_hbm, wout_ref, 4),
+        load(order_hbm, order_ref, 5),
     ]
-    for load in loads:
-        load.start()
+    for number in range(3):
+        loads[number].start()
 
     barrier = pltpu.get_barrier_semaphore()
 
@@ -202,6 +214,9 @@
     def arrive(phase):
         copies(phase).wait_recv()
 
+    for number in range(3, 6):
+        loads[number].start()
+
     head_of_row = iota((HEADS * ROWS, D), 0) >> 4
     lane = iota((HEADS * ROWS, D), 1)
     in_head = (lane >= head_of_row * HEAD) & (lane < head_of_row * HEAD + HEAD)
@@ -215,47 +230,44 @@
     pl.semaphore_wait(barrier, NP + NC - 2)
     send(0, lambda p: texts.at[s])
 
+    query = probe_ref[...].reshape(1, D).astype(BF16).astype(F32)
+    query_heads = (mask_ref[...].astype(F32) * query).astype(BF16)
     loads[1].wait()
     loads[2].wait()
-
-    def project(step, carry):
-        columns = pl.ds(pl.multiple_of(step * 256, 256), 256)
-        kv_ref[:, columns] = nn(x_ref[...], wkv_ref[:, columns]).astype(BF16)
-        return carry
-
-    lax.fori_loop(0, 2 * D // 256, project, 0)
-
-    query = probe_ref[...].astype(BF16).astype(F32)
-    query_heads = (mask_ref[...].astype(F32) * query).astype(BF16)
+    for block in range(3):
+        columns = slice(384 * block, 384 * block + 384)
+        keys_ref[:, columns] = nn(x_ref[...], wk_ref[:, columns]).astype(BF16)
+    scores = nt(keys_ref[...], query_heads) / ROOT
+
     same = (iota((ROWS * PATCH, HEADS * ROWS), 0) >> 5) == (
         iota((ROWS * PATCH, HEADS * ROWS), 1) & (ROWS - 1)
     )
-    scores = nt(kv_ref[:, :D], query_heads) / ROOT
     highest = jnp.max(jnp.where(same, scores, -jnp.inf), axis=0, keepdims=True)
     powers = jnp.where(same, jnp.exp(scores - highest), 0.0)
     weights = powers / jnp.sum(powers, axis=0, keepdims=True)
     soft_ref[...] = weights
     weights_t = weights.T.astype(BF16)
 
-    mixed = nn(weights_t, kv_ref[:, D:]) * mask_ref[...].astype(F32)
+    patch_sums = nn(weights_t, x_ref[...]).astype(BF16)
+    loads[3].wait()
+    mixed = nn(patch_sums, wv_ref[...]) * mask_ref[...].astype(F32)
     pooled = jnp.sum(mixed.reshape(HEADS, ROWS, D), axis=0)
     pooled_half = pooled.astype(BF16)
-    loads[3].wait()
+    loads[4].wait()
     image_out = nn(pooled_half, wout_ref[...])
     image_length = jnp.sqrt(jnp.sum(image_out * image_out, axis=1, keepdims=True) + 1e-06)
     image_unit = image_out / image_length
     images[c] = image_unit.astype(BF16)
     send(1, lambda p: images.at[c])
 
-    patch_sums = nn(weights_t, x_ref[...]).astype(BF16)
     features = jnp.concatenate([pooled_half, text_ref[...]], axis=0)
-    loads[4].wait()
-
+    loads[5].wait()
     for place in range(NC):
         rows = order_ref[SLAB * place : SLAB * place + SLAB, :]
         slab_out[place, :SLAB, :] = nt(rows, patch_sums).astype(BF16)
         slab_out[place, SLAB:, :SLAB] = nt(features, rows).astype(BF16)
     slab_in[c] = slab_out[c]
+    send(4, lambda p: slab_out.at[p])
 
     temperature = jnp.exp(scale_ref[...])
     arrive(0)
@@ -274,7 +286,6 @@
     iret_out[...] = nn(coeff.astype(BF16), text_all).astype(BF16).reshape(NC, ROWS, D)
     iret_in[c] = iret_out[c]
     send(3, lambda p: iret_out.at[p])
-    send(4, lambda p: slab_out.at[p])
 
     arrive(3)
     image_returned = temperature * slot_sum(iret_in, NC)
@@ -285,7 +296,7 @@
     pooled_grad = nt(image_grad, wout_ref[...]).astype(BF16).astype(F32)
     tiled = jnp.concatenate([pooled_grad] * HEADS, axis=0)
     grad_heads = (mask_ref[...].astype(F32) * tiled).astype(BF16)
-    weight_grad = nt(kv_ref[:, D:], grad_heads)
+    weight_grad = nn(x_ref[...], nt(wv_ref[...], grad_heads).astype(BF16))
     weights = soft_ref[...]
     inner = jnp.sum(weights * weight_grad, axis=0, keepdims=True)
     score_grad = (weights * (weight_grad - inner)).astype(BF16)
@@ -299,7 +310,7 @@
     head_row = iota((HEADS, D), 0)
     head_col = iota((HEADS, D), 1)
     own_head = (head_col >= head_row * HEAD) & (head_col < head_row * HEAD + HEAD)
-    probe_sum = jnp.where(own_head, nn(score_grad_t, kv_ref[:, :D]), 0.0) / ROOT
+    probe_sum = jnp.where(own_head, nn(score_grad_t, keys_ref[...]), 0.0) / ROOT
     tile_row = iota((HEADS, 128), 0)
     tile_lane = iota((HEADS, 128), 1)
     probe_tile = jnp.zeros((HEADS, 128), F32)
@@ -371,26 +382,30 @@
 
     arrive(10)
     tiny = slot_sum(tiny_in, NP)
-    gprobe_ref[...] = pltpu.roll(tiny, 128 - SPARE, 1)[:, :HEAD]
-    key_grad = lax.dot_general(
-        tiny.T[:16, :],
-        jnp.where(own_head, query, 0.0) / ROOT,
-        (((1,), (0,)), ((), ())),
-        preferred_element_type=F32,
-        precision=lax.Precision.HIGHEST,
-    )
-    gkv_ref[:, :D] = key_grad[:OWN]
+    probe_tile = pltpu.roll(tiny, 128 - SPARE, 1)
+    spread = jnp.where(iota((128, D), 0) == iota((1, D), 1) % HEAD, 1.0, 0.0)
+    probe_grad = exact(probe_tile, spread)
+    sums_ref[48:56, :] = jnp.broadcast_to(
+        jnp.sum(jnp.where(own_head, probe_grad, 0.0), axis=0, keepdims=True), (8, D)
+    )
+    sums_ref[32:48, :] = exact(tiny.T[:16, :], jnp.where(own_head, query, 0.0) / ROOT)
 
     arrive(8)
-    last_f32[:16, :] = slot_sum(last_in.at[0], NP)
+    sums_ref[:16, :] = slot_sum(last_in.at[0], NP)
     arrive(9)
-    last_f32[16:32, :] = slot_sum(last_in.at[1], NP)
-    gout_ref[...] = last_f32[:OWN, :]
-    gkv_ref[:, D:] = last_f32[OWN : 2 * OWN, :]
-    gtext_ref[...] = last_f32[2 * OWN : 3 * OWN, :]
+    sums_ref[16:32, :] = slot_sum(last_in.at[1], NP)
 
     for phase in started:
         copies(phase).wait_send()
+
+
+def part_sums(sums_ref, feat_ref, gkv_ref, gout_ref, gtext_ref, gprobe_ref, gfeat_ref):
+    gout_ref[...] = sums_ref[:OWN, :]
+    gkv_ref[:, :D] = sums_ref[32 : 32 + OWN, :]
+    gkv_ref[:, D:] = sums_ref[OWN : 2 * OWN, :]
+    gtext_ref[...] = sums_ref[2 * OWN : 3 * OWN, :]
+    gprobe_ref[...] = sums_ref[48:49, :].reshape(D)
+    gfeat_ref[...] = feat_ref[...]
 
 
 def column_order():
@@ -404,24 +419,22 @@
 def shards(patches, probe, key_value_matrix, output_weight, text, text_weight, log_scale, bias):
     vmem = pl.BlockSpec(memory_space=pltpu.VMEM)
     anywhere = pl.BlockSpec(memory_space=pl.ANY)
-    outs = pl.pallas_call(
+    sums = pl.pallas_call(
         kernel,
         out_shape=(
-            jax.ShapeDtypeStruct((OWN, 2 * D), F32),
-            jax.ShapeDtypeStruct((OWN, D), F32),
-            jax.ShapeDtypeStruct((OWN, D), F32),
-            jax.ShapeDtypeStruct((HEADS, HEAD), F32),
+            jax.ShapeDtypeStruct((56, D), F32),
             jax.ShapeDtypeStruct((ROWS, D), BF16),
         ),
         in_specs=[vmem] * 4 + [anywhere] * 5,
-        out_specs=(vmem,) * 5,
+        out_specs=(vmem,) * 2,
         scratch_shapes=[
             pltpu.VMEM((ROWS * PATCH, D), BF16),
-            pltpu.VMEM((D, 2 * D), BF16),
+            pltpu.VMEM((D, D), BF16),
+            pltpu.VMEM((ROWS * PATCH, D), BF16),
             pltpu.VMEM((D, D), BF16),
             pltpu.VMEM((D, D), BF16),
             pltpu.VMEM((D, D), BF16),
-            pltpu.VMEM((ROWS * PATCH, 2 * D), BF16),
+            pltpu.VMEM((D, D), BF16),
             pltpu.VMEM((HEADS * ROWS, D), BF16),
             pltpu.VMEM((ROWS * PATCH, HEADS * ROWS), F32),
             pltpu.VMEM((NP, ROWS, D), BF16),
@@ -443,7 +456,7 @@
             pltpu.VMEM((SLAB, D), F32),
             pltpu.VMEM((NP * 32, D), F32),
             pltpu.VMEM((NC * HEADS * ROWS, D), BF16),
-            pltpu.SemaphoreType.DMA((5,)),
+            pltpu.SemaphoreType.DMA((6,)),
             pltpu.SemaphoreType.DMA((11,)),
             pltpu.SemaphoreType.DMA((11,)),
         ],
@@ -453,7 +466,7 @@
     )(
         log_scale.reshape(1, 1),
         bias.reshape(1, 1),
-        probe.reshape(1, D),
+        probe,
         text,
         patches.reshape(ROWS * PATCH, D),
         key_value_matrix,
@@ -461,7 +474,18 @@
         text_weight,
         jnp.asarray(column_order()),
     )
-    return outs[0], outs[1], outs[2], outs[3].reshape(D), outs[4]
+    return pl.pallas_call(
+        part_sums,
+        out_shape=(
+            jax.ShapeDtypeStruct((OWN, 2 * D), F32),
+            jax.ShapeDtypeStruct((OWN, D), F32),
+            jax.ShapeDtypeStruct((OWN, D), F32),
+            jax.ShapeDtypeStruct((D,), F32),
+            jax.ShapeDtypeStruct((ROWS, D), BF16),
+        ),
+        in_specs=[vmem] * 2,
+        out_specs=(vmem,) * 5,
+    )(*sums)
 
 
 def solution(mesh):

time: 71.4 us -> 60.3 us (0.84)
  local copies, waits for them, and re-layouts: 8.68 us -> 0 us
  Pallas kernels: 60.3 us -> 58.2 us
    unnamed x4 -> x0, local copies, waits for them, and re-layouts: 6.01 us -> none
    reshape x2 -> x0, local copies, waits for them, and re-layouts: 2.67 us -> none  [the longest x1 1.38 us: shards(): return (outs[0], outs[1], outs[2], outs[3].reshape(D), outs[4])]
    pallas_call x1 -> x2, Pallas kernels: 60.3 us -> 58.2 us  [the longest x1 56.5 us: shards(): pl.pallas_call(kernel, out_shape=(jax.ShapeDtypeStruct((56, D), F32), jax...]
where the time goes in v3:
time: 60.3 us; the launch traced here: 60.1 us
  Pallas kernels  58.2 us (97%)
  between operations  1.93 us (3%)
    pallas_call x1, Pallas kernels, shards(): pl.pallas_call(kernel, out_shape=(jax.ShapeDtypeStruct((56, D), F32), jax...  56.5 us
    pallas_call x1, Pallas kernels, shards(): pl.pallas_call(part_sums, out_shape=(jax.ShapeDtypeStruct((OWN, 2 * D), F...  1.68 us

profile of v3, /device:TPU:1, one launch (start us, length us, event | category | flops | bytes accessed | tf_op | source)
XLA Modules:
  0.0 60.1 jit_solution(8559014862289725045)
XLA Ops:
  1.9 56.5 %shard_map.128 = (f32[56,1152]{1,0:T(8,128)}, bf16[16,1152]{1,0:T(8,128)(2,1)}) custom-call(f32[1,1]{1,0:T(1,128)} %bitcast.3.scale_ref, f32[1,1]{1,0:T(1,128)} %bitcast.4.bias_ref, f32[1152]{0:T(1024)} %probe_ref.1, bf16[16,1152]{1,0:T(8,128)(2,1)} %text_ref.1, bf16[512,1152]{1,0:T(8,128)(2,1)} %bitcast.5, bf16[1152,2304]{1,0:T(8,128)(2,1)} %wkv_hbm.1, ...), custom_call_target="tpu_custom_call" | custom-call | tf_op jit(solution)/shard_map/pallas_call | solution.py:422
  58.5 1.7 %shard_map.129 = (f32[9,2304]{1,0:T(8,128)}, f32[9,1152]{1,0:T(8,128)}, f32[9,1152]{1,0:T(8,128)}, f32[1152]{0:T(1024)}, bf16[16,1152]{1,0:T(8,128)(2,1)}) custom-call(f32[56,1152]{1,0:T(8,128)} %get-tuple-element.7.sums_ref, bf16[16,1152]{1,0:T(8,128)(2,1)} %get-tuple-element.8.feat_ref), custom_call_target="tpu_custom_call" | custom-call | tf_op jit(solution)/shard_map/pallas_call | solution.py:477

commit v4 on v3

--- a/solution.py
+++ b/solution.py
@@ -65,8 +65,8 @@
 
 
 def send_all(peer_of, count, me, source, target, send_sem, recv_sem):
-    def one(step, carry):
-        peer = lax.rem(me + step, count)
+    for step in range(1, count):
+        peer = (me + step) & (count - 1)
         pltpu.make_async_remote_copy(
             src_ref=source(peer),
             dst_ref=target(me),
@@ -75,9 +75,6 @@
             device_id=peer_of(peer),
             device_id_type=MESH,
         ).start()
-        return carry
-
-    lax.fori_loop(1, count, one, 0)
 
 
 def all_but_one(peer_of, count, me, target, send_sem, recv_sem):
@@ -118,6 +115,8 @@
     x_ref,
     wk_ref,
     keys_ref,
+    values_ref,
+    sorted_ref,
     wv_ref,
     wout_ref,
     wtext_ref,
@@ -146,17 +145,31 @@
     load_sem,
     send_sem,
     recv_sem,
+    share_sem,
 ):
     l = lax.axis_index("loop")
     k = lax.axis_index("grp")
-    c = (k % 2) * 4 + l % 4
-    s = (l // 4) * 4 + k // 2
+    c = (l & 1) * 4 + (k & 1) * 2 + ((l >> 1) & 1)
+    s = (l & 12) + (k >> 1)
 
     def in_column(peer):
-        return {"loop": (l // 4) * 4 + peer % 4, "grp": (k // 2) * 2 + peer // 4}
+        return {
+            "loop": (l & 12) + (peer & 1) * 2 + (peer >> 2),
+            "grp": (k & 6) + ((peer >> 1) & 1),
+        }
 
     def in_plane(peer):
-        return {"loop": (peer // 4) * 4 + l % 4, "grp": (peer % 4) * 2 + k % 2}
+        return {"loop": (peer & 12) + (l & 3), "grp": (peer & 3) * 2 + (k & 1)}
+
+    barrier = pltpu.get_barrier_semaphore()
+    for peer_of, count, me in ((in_plane, NP, s), (in_column, NC, c)):
+        for step in range(1, count):
+            pl.semaphore_signal(
+                barrier,
+                inc=1,
+                device_id=peer_of((me + step) & (count - 1)),
+                device_id_type=MESH,
+            )
 
     def load(source, target, number):
         return pltpu.make_async_copy(source, target, load_sem.at[number])
@@ -171,19 +184,6 @@
     ]
     for number in range(3):
         loads[number].start()
-
-    barrier = pltpu.get_barrier_semaphore()
-
-    def greet(peer_of, count, me):
-        def one(step, carry):
-            peer = peer_of(lax.rem(me + step, count))
-            pl.semaphore_signal(barrier, inc=1, device_id=peer, device_id_type=MESH)
-            return carry
-
-        lax.fori_loop(1, count, one, 0)
-
-    greet(in_plane, NP, s)
-    greet(in_column, NC, c)
 
     column = (in_column, NC, c)
     plane = (in_plane, NP, s)
@@ -211,11 +211,32 @@
         send_all(peer_of, count, me, source, target, send_sem.at[phase], recv_sem.at[phase])
         started.append(phase)
 
+    def block_copy(phase, slots, peer, number):
+        block = phases[phase][1](slots)
+        return pltpu.make_async_remote_copy(
+            src_ref=block,
+            dst_ref=block,
+            send_sem=send_sem.at[phase],
+            recv_sem=share_sem.at[phase, number],
+            device_id=in_column(peer),
+            device_id_type=MESH,
+        )
+
+    def share(phase):
+        for step in (2, 1, 3):
+            block_copy(phase, c, (c & 4) + ((c + step) & 3), step).start()
+        block_copy(phase, c, c ^ 4, 0).start()
+        started.append(phase)
+
+    def arrive_shared(phase):
+        for step in (1, 3, 2):
+            slot = (c & 4) + ((c - step) & 3)
+            block_copy(phase, slot, c ^ 4, step).wait_recv()
+            block_copy(phase, slot, c ^ 4, 0).start()
+        block_copy(phase, pl.ds((c & 4) ^ 4, 4), c ^ 4, 0).wait_recv()
+
     def arrive(phase):
         copies(phase).wait_recv()
-
-    for number in range(3, 6):
-        loads[number].start()
 
     head_of_row = iota((HEADS * ROWS, D), 0) >> 4
     lane = iota((HEADS * ROWS, D), 1)
@@ -223,17 +244,18 @@
     mask_ref[...] = jnp.where(in_head, 1.0, 0.0).astype(BF16)
 
     loads[0].wait()
+    loads[3].start()
     text_out = nn(text_ref[...], wtext_ref[...])
     text_length = jnp.sqrt(jnp.sum(text_out * text_out, axis=1, keepdims=True) + 1e-06)
     text_unit = text_out / text_length
     texts[s] = text_unit.astype(BF16)
-    pl.semaphore_wait(barrier, NP + NC - 2)
-    send(0, lambda p: texts.at[s])
 
     query = probe_ref[...].reshape(1, D).astype(BF16).astype(F32)
     query_heads = (mask_ref[...].astype(F32) * query).astype(BF16)
     loads[1].wait()
     loads[2].wait()
+    loads[4].start()
+    loads[5].start()
     for block in range(3):
         columns = slice(384 * block, 384 * block + 384)
         keys_ref[:, columns] = nn(x_ref[...], wk_ref[:, columns]).astype(BF16)
@@ -246,6 +268,9 @@
     powers = jnp.where(same, jnp.exp(scores - highest), 0.0)
     weights = powers / jnp.sum(powers, axis=0, keepdims=True)
     soft_ref[...] = weights
+    pl.semaphore_wait(barrier, NP + NC - 2)
+    send(0, lambda p: texts.at[s])
+
     weights_t = weights.T.astype(BF16)
 
     patch_sums = nn(weights_t, x_ref[...]).astype(BF16)
@@ -258,20 +283,22 @@
     image_length = jnp.sqrt(jnp.sum(image_out * image_out, axis=1, keepdims=True) + 1e-06)
     image_unit = image_out / image_length
     images[c] = image_unit.astype(BF16)
-    send(1, lambda p: images.at[c])
+    share(1)
 
     features = jnp.concatenate([pooled_half, text_ref[...]], axis=0)
     loads[5].wait()
+    slab_out[:, :SLAB, :] = nt(order_ref[...], patch_sums).astype(BF16).reshape(
+        NC, SLAB, HEADS * ROWS
+    )
     for place in range(NC):
         rows = order_ref[SLAB * place : SLAB * place + SLAB, :]
-        slab_out[place, :SLAB, :] = nt(rows, patch_sums).astype(BF16)
         slab_out[place, SLAB:, :SLAB] = nt(features, rows).astype(BF16)
     slab_in[c] = slab_out[c]
     send(4, lambda p: slab_out.at[p])
 
     temperature = jnp.exp(scale_ref[...])
     arrive(0)
-    arrive(1)
+    arrive_shared(1)
     text_all = texts[...].reshape(NP * ROWS, D)
     image_all = images[...].reshape(NC * ROWS, D)
     logits = temperature * nt(image_all, text_all) + bias_ref[...]
@@ -280,33 +307,41 @@
     matched = ((row >> 4) == c) & ((col >> 4) == s) & ((row & 15) == (col & 15))
     sign = jnp.where(matched, 1.0, -1.0)
     coeff = -sign / (1.0 + jnp.exp(sign * logits))
+    iret_out[...] = nn(coeff.astype(BF16), text_all).astype(BF16).reshape(NC, ROWS, D)
+    iret_in[c] = iret_out[c]
+    send(3, lambda p: iret_out.at[p])
     tret_out[...] = nn(flip(coeff), image_all).astype(BF16).reshape(NP, ROWS, D)
     tret_in[s] = tret_out[s]
     send(2, lambda p: tret_out.at[p])
-    iret_out[...] = nn(coeff.astype(BF16), text_all).astype(BF16).reshape(NC, ROWS, D)
-    iret_in[c] = iret_out[c]
-    send(3, lambda p: iret_out.at[p])
+
+    for block in range(3):
+        columns = slice(384 * block, 384 * block + 384)
+        values_ref[:, columns] = nn(x_ref[...], wv_ref[:, columns]).astype(BF16)
+        sorted_ref[:, columns] = nt(x_ref[...], order_ref[columns, :]).astype(BF16)
 
     arrive(3)
     image_returned = temperature * slot_sum(iret_in, NC)
     image_grad = unit_backward(image_returned, image_unit, image_length).astype(BF16)
     igo_all[c] = image_grad
-    send(5, lambda p: igo_all.at[c])
+    share(5)
 
     pooled_grad = nt(image_grad, wout_ref[...]).astype(BF16).astype(F32)
     tiled = jnp.concatenate([pooled_grad] * HEADS, axis=0)
     grad_heads = (mask_ref[...].astype(F32) * tiled).astype(BF16)
-    weight_grad = nn(x_ref[...], nt(wv_ref[...], grad_heads).astype(BF16))
+    weight_grad = nt(values_ref[...], grad_heads)
     weights = soft_ref[...]
     inner = jnp.sum(weights * weight_grad, axis=0, keepdims=True)
     score_grad = (weights * (weight_grad - inner)).astype(BF16)
     fold = jnp.where((iota((HEADS * ROWS, 128), 0) >> 4) == iota((HEADS * ROWS, 128), 1), 1.0, 0.0)
     score_grad_t = nn(score_grad, fold.astype(BF16)).T[:HEADS].astype(BF16)
 
-    key_sum = nn(score_grad_t, x_ref[...])
-    high = key_sum.astype(BF16)
-    low = (key_sum - high.astype(F32)).astype(BF16)
-    key_sum = jnp.concatenate([high, low], axis=0)
+    arrive(2)
+    text_returned = temperature * slot_sum(tret_in, NP)
+    text_grad = unit_backward(text_returned, text_unit, text_length).astype(BF16)
+    tgo_all[c] = text_grad
+    share(6)
+
+    key_sum = nn(score_grad_t, sorted_ref[...])
     head_row = iota((HEADS, D), 0)
     head_col = iota((HEADS, D), 1)
     own_head = (head_col >= head_row * HEAD) & (head_col < head_row * HEAD + HEAD)
@@ -318,20 +353,13 @@
         probe_tile = jnp.where(tile_row == head, slab_of(probe_sum, HEAD * head), probe_tile)
     probe_tile = pltpu.roll(probe_tile, SPARE, 1)
     for place in range(NC):
-        rows = order_ref[SLAB * place : SLAB * place + SLAB, :]
-        split = nt(key_sum, rows)
-        small_out[place, :, :SLAB] = split[:HEADS] + split[HEADS:]
+        start = SLAB * place
+        small_out[place, :, :128] = slab_of(key_sum, start)
         small_out[place, :, 128:] = jnp.where(
-            tile_lane < SPARE, small_out[place, :, 128:], probe_tile
+            tile_lane < SPARE, slab_of(key_sum, start + 128), probe_tile
         )
     small_in[c] = small_out[c]
     send(7, lambda p: small_out.at[p])
-
-    arrive(2)
-    text_returned = temperature * slot_sum(tret_in, NP)
-    text_grad = unit_backward(text_returned, text_unit, text_length).astype(BF16)
-    tgo_all[c] = text_grad
-    send(6, lambda p: tgo_all.at[c])
 
     last_f32[...] = jnp.zeros_like(last_f32)
 
@@ -342,7 +370,7 @@
             ]
 
     arrive(4)
-    arrive(5)
+    arrive_shared(5)
     igo = igo_all[...].reshape(NC * ROWS, D)
     part_ref[...] = nn(flip(slab_in[:, SLAB : SLAB + ROWS, :].reshape(NC * ROWS, 256))[:SLAB], igo)
     place_rows(0)
@@ -371,7 +399,7 @@
     tiny_in[s] = tiny_out[s]
     send(10, lambda p: tiny_out.at[p])
 
-    arrive(6)
+    arrive_shared(6)
     tgo = tgo_all[...].reshape(NC * ROWS, D)
     part_ref[...] = nn(flip(slab_in[:, SLAB + ROWS :, :].reshape(NC * ROWS, 256))[:SLAB], tgo)
     place_rows(2 * OWN)
@@ -410,8 +438,8 @@
 
 def column_order():
     c, s, r = np.meshgrid(np.arange(NC), np.arange(NP), np.arange(OWN), indexing="ij")
-    loop = (s // 4) * 4 + c % 4
-    grp = (s % 4) * 2 + c // 4
+    loop = (s // 4) * 4 + (c % 2) * 2 + c // 4
+    grp = (s % 4) * 2 + c // 2 % 2
     kept = ((loop * 8 + grp) * OWN + r).reshape(D)
     return (kept[:, None] == np.arange(D)[None, :]).astype(ml_dtypes.bfloat16)
 
@@ -430,6 +458,8 @@
         scratch_shapes=[
             pltpu.VMEM((ROWS * PATCH, D), BF16),
             pltpu.VMEM((D, D), BF16),
+            pltpu.VMEM((ROWS * PATCH, D), BF16),
+            pltpu.VMEM((ROWS * PATCH, D), BF16),
             pltpu.VMEM((ROWS * PATCH, D), BF16),
             pltpu.VMEM((D, D), BF16),
             pltpu.VMEM((D, D), BF16),
@@ -459,6 +489,7 @@
             pltpu.SemaphoreType.DMA((6,)),
             pltpu.SemaphoreType.DMA((11,)),
             pltpu.SemaphoreType.DMA((11,)),
+            pltpu.SemaphoreType.DMA((11, 4)),
         ],
         compiler_params=pltpu.CompilerParams(
             collective_id=0, has_side_effects=True, vmem_limit_bytes=56 * 1024 * 1024

time: 60.3 us -> 57.8 us (0.959)
  Pallas kernels: 58.2 us -> 55.6 us
    pallas_call x1, Pallas kernels: 56.5 us -> 54 us  [shards(): pl.pallas_call(kernel, out_shape=(jax.ShapeDtypeStruct((56, D), F32), jax...]
where the time goes in v4:
time: 57.8 us; the launch traced here: 57.6 us
  Pallas kernels  55.6 us (96%)
  between operations  1.93 us (3%)
    pallas_call x1, Pallas kernels, shards(): pl.pallas_call(kernel, out_shape=(jax.ShapeDtypeStruct((56, D), F32), jax...  54 us
    pallas_call x1, Pallas kernels, shards(): pl.pallas_call(part_sums, out_shape=(jax.ShapeDtypeStruct((OWN, 2 * D), F...  1.68 us

profile of v4, /device:TPU:1, one launch (start us, length us, event | category | flops | bytes accessed | tf_op | source)
XLA Modules:
  0.0 57.6 jit_solution(4199925174268916701)
XLA Ops:
  1.9 54.0 %shard_map.128 = (f32[56,1152]{1,0:T(8,128)}, bf16[16,1152]{1,0:T(8,128)(2,1)}) custom-call(f32[1,1]{1,0:T(1,128)} %bitcast.3.scale_ref, f32[1,1]{1,0:T(1,128)} %bitcast.4.bias_ref, f32[1152]{0:T(1024)} %probe_ref.1, bf16[16,1152]{1,0:T(8,128)(2,1)} %text_ref.1, bf16[512,1152]{1,0:T(8,128)(2,1)} %bitcast.5, bf16[1152,2304]{1,0:T(8,128)(2,1)} %wkv_hbm.1, ...), custom_call_target="tpu_custom_call" | custom-call | tf_op jit(solution)/shard_map/pallas_call | solution.py:450
  55.9 1.7 %shard_map.129 = (f32[9,2304]{1,0:T(8,128)}, f32[9,1152]{1,0:T(8,128)}, f32[9,1152]{1,0:T(8,128)}, f32[1152]{0:T(1024)}, bf16[16,1152]{1,0:T(8,128)(2,1)}) custom-call(f32[56,1152]{1,0:T(8,128)} %get-tuple-element.7.sums_ref, bf16[16,1152]{1,0:T(8,128)(2,1)} %get-tuple-element.8.feat_ref), custom_call_target="tpu_custom_call" | custom-call | tf_op jit(solution)/shard_map/pallas_call | solution.py:508

commit v5 on v4

--- a/solution.py
+++ b/solution.py
@@ -119,6 +119,7 @@
     sorted_ref,
     wv_ref,
     wout_ref,
+    wout_t_ref,
     wtext_ref,
     order_ref,
     mask_ref,
@@ -127,7 +128,11 @@
     images,
     slab_out,
     slab_in,
+    feat_out,
+    feat_in,
     iret_out,
+    iret_half,
+    iret_sum,
     iret_in,
     tret_out,
     tret_in,
@@ -146,6 +151,7 @@
     send_sem,
     recv_sem,
     share_sem,
+    quarter_sem,
 ):
     l = lax.axis_index("loop")
     k = lax.axis_index("grp")
@@ -191,7 +197,6 @@
         0: (plane, lambda i: texts.at[i]),
         1: (column, lambda i: images.at[i]),
         2: (plane, lambda i: tret_in.at[i]),
-        3: (column, lambda i: iret_in.at[i]),
         4: (column, lambda i: slab_in.at[i]),
         5: (column, lambda i: igo_all.at[i]),
         6: (column, lambda i: tgo_all.at[i]),
@@ -199,6 +204,7 @@
         8: (plane, lambda i: last_in.at[0, i]),
         9: (plane, lambda i: last_in.at[1, i]),
         10: (plane, lambda i: tiny_in.at[i]),
+        11: (column, lambda i: feat_in.at[i]),
     }
     started = []
 
@@ -259,6 +265,9 @@
     for block in range(3):
         columns = slice(384 * block, 384 * block + 384)
         keys_ref[:, columns] = nn(x_ref[...], wk_ref[:, columns]).astype(BF16)
+        if block == 1:
+            pl.semaphore_wait(barrier, NP + NC - 2)
+            send(0, lambda p: texts.at[s])
     scores = nt(keys_ref[...], query_heads) / ROOT
 
     same = (iota((ROWS * PATCH, HEADS * ROWS), 0) >> 5) == (
@@ -268,9 +277,6 @@
     powers = jnp.where(same, jnp.exp(scores - highest), 0.0)
     weights = powers / jnp.sum(powers, axis=0, keepdims=True)
     soft_ref[...] = weights
-    pl.semaphore_wait(barrier, NP + NC - 2)
-    send(0, lambda p: texts.at[s])
-
     weights_t = weights.T.astype(BF16)
 
     patch_sums = nn(weights_t, x_ref[...]).astype(BF16)
@@ -285,16 +291,20 @@
     images[c] = image_unit.astype(BF16)
     share(1)
 
+    loads[5].wait()
+    slab_out[...] = nt(order_ref[...], patch_sums).astype(BF16).reshape(NC, SLAB, HEADS * ROWS)
+    slab_in[c] = slab_out[c]
+    send(4, lambda p: slab_out.at[p])
     features = jnp.concatenate([pooled_half, text_ref[...]], axis=0)
-    loads[5].wait()
-    slab_out[:, :SLAB, :] = nt(order_ref[...], patch_sums).astype(BF16).reshape(
-        NC, SLAB, HEADS * ROWS
-    )
     for place in range(NC):
         rows = order_ref[SLAB * place : SLAB * place + SLAB, :]
-        slab_out[place, SLAB:, :SLAB] = nt(features, rows).astype(BF16)
-    slab_in[c] = slab_out[c]
-    send(4, lambda p: slab_out.at[p])
+        feat_out[place, :, :SLAB] = nt(features, rows).astype(BF16)
+    feat_in[c] = feat_out[c]
+    send(11, lambda p: feat_out.at[p])
+
+    for block in range(3):
+        rows = slice(384 * block, 384 * block + 384)
+        wout_t_ref[:, rows] = flip(wout_ref[rows, :])
 
     temperature = jnp.exp(scale_ref[...])
     arrive(0)
@@ -308,24 +318,52 @@
     sign = jnp.where(matched, 1.0, -1.0)
     coeff = -sign / (1.0 + jnp.exp(sign * logits))
     iret_out[...] = nn(coeff.astype(BF16), text_all).astype(BF16).reshape(NC, ROWS, D)
-    iret_in[c] = iret_out[c]
-    send(3, lambda p: iret_out.at[p])
+    halves = pltpu.make_async_remote_copy(
+        src_ref=iret_out.at[pl.ds((c & 4) ^ 4, 4)],
+        dst_ref=iret_half,
+        send_sem=send_sem.at[3],
+        recv_sem=recv_sem.at[3],
+        device_id=in_column(c ^ 4),
+        device_id_type=MESH,
+    )
+    halves.start()
     tret_out[...] = nn(flip(coeff), image_all).astype(BF16).reshape(NP, ROWS, D)
     tret_in[s] = tret_out[s]
     send(2, lambda p: tret_out.at[p])
+    halves.wait_recv()
+    iret_sum[...] = (
+        iret_out[pl.ds(c & 4, 4)].astype(F32) + iret_half[...].astype(F32)
+    ).astype(BF16)
+    iret_in[c & 3] = iret_sum[c & 3]
+
+    def quarter(step, slot):
+        return pltpu.make_async_remote_copy(
+            src_ref=iret_sum.at[slot],
+            dst_ref=iret_in.at[c & 3],
+            send_sem=quarter_sem.at[0, step],
+            recv_sem=quarter_sem.at[1, step],
+            device_id=in_column((c & 4) + slot),
+            device_id_type=MESH,
+        )
+
+    quarters = [quarter(step, (c + step) & 3) for step in (2, 1, 3)]
+    for copy in quarters:
+        copy.start()
 
     for block in range(3):
         columns = slice(384 * block, 384 * block + 384)
         values_ref[:, columns] = nn(x_ref[...], wv_ref[:, columns]).astype(BF16)
         sorted_ref[:, columns] = nt(x_ref[...], order_ref[columns, :]).astype(BF16)
-
-    arrive(3)
-    image_returned = temperature * slot_sum(iret_in, NC)
+    last_f32[...] = jnp.zeros_like(last_f32)
+
+    for copy in quarters:
+        copy.wait_recv()
+    image_returned = temperature * slot_sum(iret_in, 4)
     image_grad = unit_backward(image_returned, image_unit, image_length).astype(BF16)
     igo_all[c] = image_grad
     share(5)
 
-    pooled_grad = nt(image_grad, wout_ref[...]).astype(BF16).astype(F32)
+    pooled_grad = nn(image_grad, wout_t_ref[...]).astype(BF16).astype(F32)
     tiled = jnp.concatenate([pooled_grad] * HEADS, axis=0)
     grad_heads = (mask_ref[...].astype(F32) * tiled).astype(BF16)
     weight_grad = nt(values_ref[...], grad_heads)
@@ -361,7 +399,6 @@
     small_in[c] = small_out[c]
     send(7, lambda p: small_out.at[p])
 
-    last_f32[...] = jnp.zeros_like(last_f32)
 
     def place_rows(offset):
         for part in range(NP):
@@ -369,16 +406,17 @@
                 OWN * part : OWN * part + OWN, :
             ]
 
-    arrive(4)
+    arrive(11)
     arrive_shared(5)
     igo = igo_all[...].reshape(NC * ROWS, D)
-    part_ref[...] = nn(flip(slab_in[:, SLAB : SLAB + ROWS, :].reshape(NC * ROWS, 256))[:SLAB], igo)
+    part_ref[...] = nn(flip(feat_in[:, :ROWS, :].reshape(NC * ROWS, 256))[:SLAB], igo)
     place_rows(0)
-    pooled_grads = nt(igo, wout_ref[...]).astype(BF16)
+    pooled_grads = nn(igo, wout_t_ref[...]).astype(BF16)
     for place in range(NC):
         tiled = jnp.concatenate([pooled_grads[ROWS * place : ROWS * place + ROWS]] * HEADS, axis=0)
         heads_ref[256 * place : 256 * place + 256, :] = mask_ref[...] * tiled
-    left = jnp.concatenate([slab_in[place, :SLAB, :] for place in range(NC)], axis=1)
+    arrive(4)
+    left = jnp.concatenate([slab_in[place] for place in range(NC)], axis=1)
     part_ref[...] = nn(left, heads_ref[...])
     place_rows(OWN)
 
@@ -390,6 +428,11 @@
     pack(0)
     send(8, lambda p: last_out.at[0, p])
 
+    arrive_shared(6)
+    tgo = tgo_all[...].reshape(NC * ROWS, D)
+    part_ref[...] = nn(flip(feat_in[:, ROWS:, :].reshape(NC * ROWS, 256))[:SLAB], tgo)
+    place_rows(2 * OWN)
+    pack(1)
     arrive(7)
     tiny = slot_sum(small_in, NC)
     for place in range(NP):
@@ -399,11 +442,6 @@
     tiny_in[s] = tiny_out[s]
     send(10, lambda p: tiny_out.at[p])
 
-    arrive_shared(6)
-    tgo = tgo_all[...].reshape(NC * ROWS, D)
-    part_ref[...] = nn(flip(slab_in[:, SLAB + ROWS :, :].reshape(NC * ROWS, 256))[:SLAB], tgo)
-    place_rows(2 * OWN)
-    pack(1)
     send(9, lambda p: last_out.at[1, p])
 
     gfeat_ref[...] = nt(text_grad, wtext_ref[...]).astype(BF16)
@@ -423,6 +461,8 @@
     arrive(9)
     sums_ref[16:32, :] = slot_sum(last_in.at[1], NP)
 
+    for copy in [halves] + quarters:
+        copy.wait_send()
     for phase in started:
         copies(phase).wait_send()
 
@@ -465,14 +505,19 @@
             pltpu.VMEM((D, D), BF16),
             pltpu.VMEM((D, D), BF16),
             pltpu.VMEM((D, D), BF16),
+            pltpu.VMEM((D, D), BF16),
             pltpu.VMEM((HEADS * ROWS, D), BF16),
             pltpu.VMEM((ROWS * PATCH, HEADS * ROWS), F32),
             pltpu.VMEM((NP, ROWS, D), BF16),
             pltpu.VMEM((NC, ROWS, D), BF16),
-            pltpu.VMEM((NC, SLAB + 2 * ROWS, HEADS * ROWS), BF16),
-            pltpu.VMEM((NC, SLAB + 2 * ROWS, HEADS * ROWS), BF16),
+            pltpu.VMEM((NC, SLAB, HEADS * ROWS), BF16),
+            pltpu.VMEM((NC, SLAB, HEADS * ROWS), BF16),
+            pltpu.VMEM((NC, 2 * ROWS, HEADS * ROWS), BF16),
+            pltpu.VMEM((NC, 2 * ROWS, HEADS * ROWS), BF16),
             pltpu.VMEM((NC, ROWS, D), BF16),
-            pltpu.VMEM((NC, ROWS, D), BF16),
+            pltpu.VMEM((4, ROWS, D), BF16),
+            pltpu.VMEM((4, ROWS, D), BF16),
+            pltpu.VMEM((4, ROWS, D), BF16),
             pltpu.VMEM((NP, ROWS, D), BF16),
             pltpu.VMEM((NP, ROWS, D), BF16),
             pltpu.VMEM((NC, ROWS, D), BF16),
@@ -487,9 +532,10 @@
             pltpu.VMEM((NP * 32, D), F32),
             pltpu.VMEM((NC * HEADS * ROWS, D), BF16),
             pltpu.SemaphoreType.DMA((6,)),
-            pltpu.SemaphoreType.DMA((11,)),
-            pltpu.SemaphoreType.DMA((11,)),
+            pltpu.SemaphoreType.DMA((12,)),
+            pltpu.SemaphoreType.DMA((12,)),
             pltpu.SemaphoreType.DMA((11, 4)),
+            pltpu.SemaphoreType.DMA((2, 4)),
         ],
         compiler_params=pltpu.CompilerParams(
             collective_id=0, has_side_effects=True, vmem_limit_bytes=56 * 1024 * 1024

time: 57.8 us -> 56.3 us (0.974)
  Pallas kernels: 55.6 us -> 54.2 us
    pallas_call x1, Pallas kernels: 54 us -> 52.5 us  [shards(): pl.pallas_call(kernel, out_shape=(jax.ShapeDtypeStruct((56, D), F32), jax...]
where the time goes in v5:
time: 56.3 us; the launch traced here: 56.1 us
  Pallas kernels  54.2 us (96%)
  between operations  1.93 us (3%)
    pallas_call x1, Pallas kernels, shards(): pl.pallas_call(kernel, out_shape=(jax.ShapeDtypeStruct((56, D), F32), jax...  52.5 us
    pallas_call x1, Pallas kernels, shards(): pl.pallas_call(part_sums, out_shape=(jax.ShapeDtypeStruct((OWN, 2 * D), F...  1.68 us

profile of v5, /device:TPU:1, one launch (start us, length us, event | category | flops | bytes accessed | tf_op | source)
XLA Modules:
  0.0 56.1 jit_solution(10013262676612602398)
XLA Ops:
  1.9 52.5 %shard_map.128 = (f32[56,1152]{1,0:T(8,128)}, bf16[16,1152]{1,0:T(8,128)(2,1)}) custom-call(f32[1,1]{1,0:T(1,128)} %bitcast.3.scale_ref, f32[1,1]{1,0:T(1,128)} %bitcast.4.bias_ref, f32[1152]{0:T(1024)} %probe_ref.1, bf16[16,1152]{1,0:T(8,128)(2,1)} %text_ref.1, bf16[512,1152]{1,0:T(8,128)(2,1)} %bitcast.5, bf16[1152,2304]{1,0:T(8,128)(2,1)} %wkv_hbm.1, ...), custom_call_target="tpu_custom_call" | custom-call | tf_op jit(solution)/shard_map/pallas_call | solution.py:490
  54.4 1.7 %shard_map.129 = (f32[9,2304]{1,0:T(8,128)}, f32[9,1152]{1,0:T(8,128)}, f32[9,1152]{1,0:T(8,128)}, f32[1152]{0:T(1024)}, bf16[16,1152]{1,0:T(8,128)(2,1)}) custom-call(f32[56,1152]{1,0:T(8,128)} %get-tuple-element.7.sums_ref, bf16[16,1152]{1,0:T(8,128)(2,1)} %get-tuple-element.8.feat_ref), custom_call_target="tpu_custom_call" | custom-call | tf_op jit(solution)/shard_map/pallas_call | solution.py:554

commit v6 on v5

--- a/solution.py
+++ b/solution.py
@@ -307,8 +307,8 @@
         wout_t_ref[:, rows] = flip(wout_ref[rows, :])
 
     temperature = jnp.exp(scale_ref[...])
+    arrive_shared(1)
     arrive(0)
-    arrive_shared(1)
     text_all = texts[...].reshape(NP * ROWS, D)
     image_all = images[...].reshape(NC * ROWS, D)
     logits = temperature * nt(image_all, text_all) + bias_ref[...]

time: 56.3 us -> 56.5 us (level)
  no operation moved by 1% of the time
where the time goes in v6:
time: 56.5 us; the launch traced here: 56.3 us
  Pallas kernels  54.4 us (96%)
  between operations  1.93 us (3%)
    pallas_call x1, Pallas kernels, shards(): pl.pallas_call(kernel, out_shape=(jax.ShapeDtypeStruct((56, D), F32), jax...  52.7 us
    pallas_call x1, Pallas kernels, shards(): pl.pallas_call(part_sums, out_shape=(jax.ShapeDtypeStruct((OWN, 2 * D), F...  1.68 us

profile of v6, /device:TPU:1, one launch (start us, length us, event | category | flops | bytes accessed | tf_op | source)
XLA Modules:
  0.0 56.3 jit_solution(13687934373702423228)
XLA Ops:
  1.9 52.7 %shard_map.128 = (f32[56,1152]{1,0:T(8,128)}, bf16[16,1152]{1,0:T(8,128)(2,1)}) custom-call(f32[1,1]{1,0:T(1,128)} %bitcast.3.scale_ref, f32[1,1]{1,0:T(1,128)} %bitcast.4.bias_ref, f32[1152]{0:T(1024)} %probe_ref.1, bf16[16,1152]{1,0:T(8,128)(2,1)} %text_ref.1, bf16[512,1152]{1,0:T(8,128)(2,1)} %bitcast.5, bf16[1152,2304]{1,0:T(8,128)(2,1)} %wkv_hbm.1, ...), custom_call_target="tpu_custom_call" | custom-call | tf_op jit(solution)/shard_map/pallas_call | solution.py:490
  54.6 1.7 %shard_map.129 = (f32[9,2304]{1,0:T(8,128)}, f32[9,1152]{1,0:T(8,128)}, f32[9,1152]{1,0:T(8,128)}, f32[1152]{0:T(1024)}, bf16[16,1152]{1,0:T(8,128)(2,1)}) custom-call(f32[56,1152]{1,0:T(8,128)} %get-tuple-element.7.sums_ref, bf16[16,1152]{1,0:T(8,128)(2,1)} %get-tuple-element.8.feat_ref), custom_call_target="tpu_custom_call" | custom-call | tf_op jit(solution)/shard_map/pallas_call | solution.py:554
